TPU v7x, 128 devices: a whole 4x4x4 slice. The times are simulated.
128 devices in a mesh: tiles: 128 (over z, x, y, core).
Axes of the slice: x: 4, y: 4, z: 4, core: 2. Of those that a mesh axis runs over, the one named last changes fastest.
Arguments:
- fields: bfloat16 [192, 8, 16384], P(None, None, 'tiles'), may hold values from -6 to 6
- cotangent: bfloat16 [192, 8, 16384], P(None, None, 'tiles'), may hold values from -6 to 6
- weights: bfloat16 [3, 9, 192, 192], replicated, may hold values from -0.21875 to 0.21875
- biases: float32 [3, 192], replicated, may hold values from -3 to 3
- ocean_tiles: int32 [1, 128], P(None, 'tiles'), may hold values 0 or 1
- velocity_mask: int32 [192], replicated, may hold values 0 or 1
Outputs:
- output: bfloat16 [192, 8, 16384], P(None, None, 'tiles')
- field_grad: bfloat16 [192, 8, 16384], P(None, None, 'tiles')
- weight_grad: float32 [3, 9, 192, 192], replicated
- bias_grad: float32 [3, 192], replicated
All inputs are finite; a program needn't handle non-finite values. No bound on the sum of `ocean_tiles` on one device may be relied on, other than what follows from the above.
Results may differ from a plain program's by a relative error of at most 0.011.
Values may be sent and summed in bfloat16 or wider, within the bound.
A program may use at most 128 MiB of HBM per device.

v0:
```python
import functools

import jax
import jax.numpy as jnp
from jax import lax
from jax.experimental import pallas as pl
from jax.experimental.pallas import tpu as pltpu
from jax.sharding import PartitionSpec as P

C = 192
ROWS = 8
LANES = 128
CELLS = ROWS * LANES
WIDE = 640
TOTAL = 2048
HALF = TOTAL // 2
BAND = C // 4
PART = HALF // 4
BF = jnp.bfloat16
F32 = jnp.float32
MESH = pl.DeviceIdType.MESH

CORE = (1, 2)
Y = (2, 4)
X = (8, 4)
Z = (32, 4)
ORDERS = ((Y, X, Z), (Z, Y, X), (X, Z, Y))


def coordinate(me, axis):
    return lax.rem(lax.div(me, axis[0]), axis[1])


def with_coordinate(me, axis, value):
    return me + (value - coordinate(me, axis)) * axis[0]


def copy_to(src, dst, send_sem, recv_sem, device):
    return pltpu.make_async_remote_copy(
        src_ref=src,
        dst_ref=dst,
        send_sem=send_sem,
        recv_sem=recv_sem,
        device_id=(device,),
        device_id_type=MESH,
    )


def start_if(condition, copy):
    @pl.when(condition)
    def _():
        copy.start()


def dot(a, b):
    return jnp.dot(a, b, preferred_element_type=F32)


def dot_nt(a, b):
    return lax.dot_general(a, b, (((1,), (1,)), ((), ())), preferred_element_type=F32)


def kernel(
    n,
    x_ref,
    ct_ref,
    w_ref,
    cols_ref,
    out_ref,
    fg_ref,
    dw_ref,
    s0,
    s1,
    s2,
    t0,
    t1,
    t2,
    slope,
    acc,
    grad,
    wf,
    wt,
    packed,
    turned,
    rims,
    partial,
    to_mate,
    from_mate,
    a_out,
    a_in,
    b_out,
    b_in,
    c_in,
    full,
    ex_send,
    ex_recv,
    ar_send,
    ar_recv,
):
    me = lax.axis_index("tiles")
    east = lax.rem(me + 1, n)
    west = lax.rem(me + n - 1, n)
    mirror = n - 1 - me
    fold_a = lax.rem(n - me, n)
    fold_b = lax.rem(2 * n - 2 - me, n)
    mate = with_coordinate(me, CORE, 1 - coordinate(me, CORE))
    core = coordinate(me, CORE)
    a_away = fold_a != me
    b_away = fold_b != me

    barrier = pltpu.get_barrier_semaphore()
    partners = [east, west, mirror, mate]
    for axis in (Y, X, Z):
        for step in (1, 2, 3):
            partners.append(
                with_coordinate(me, axis, lax.rem(coordinate(me, axis) + step, axis[1]))
            )
    for partner in partners:
        pl.semaphore_signal(barrier, inc=1, device_id=(partner,), device_id_type=MESH)

    @pl.when(a_away)
    def _():
        pl.semaphore_signal(barrier, inc=1, device_id=(fold_a,), device_id_type=MESH)

    @pl.when(b_away)
    def _():
        pl.semaphore_signal(barrier, inc=1, device_id=(fold_b,), device_id_type=MESH)

    lane = lax.broadcasted_iota(jnp.int32, (C, LANES), 1)
    flip_matrix = (
        lax.broadcasted_iota(jnp.int32, (LANES, LANES), 0)
        + lax.broadcasted_iota(jnp.int32, (LANES, LANES), 1)
        == LANES - 1
    ).astype(F32).astype(BF)
    flip_sign = cols_ref[:, 3:4]
    mask = cols_ref[:, 4:5]
    sends = []

    def columns(row):
        return slice(row * LANES, (row + 1) * LANES)

    def send_rims(e, buf, d, signed):
        pack = jnp.zeros((C, LANES), F32)
        for k in range(d):
            turn = dot(buf[C : 2 * C, columns(ROWS - 1 - k)], flip_matrix)
            if signed:
                turn = turn * flip_sign
            turned[e, :, columns(k)] = turn.astype(BF)
            at = 2 * d * (ROWS + k)
            here = jnp.logical_and(lane >= at, lane < at + 2 * d)
            pack = jnp.where(here, pltpu.roll(turn, (at + d) % LANES, 1), pack)
        if e == 0:
            pl.semaphore_wait(
                barrier,
                len(partners) + a_away.astype(jnp.int32) + b_away.astype(jnp.int32),
            )

        fold = copy_to(
            turned.at[e, :, pl.ds(0, d * LANES)],
            buf.at[pl.ds(C, C), pl.ds(CELLS, d * LANES)],
            ex_send.at[e, 4],
            ex_recv.at[e, 4],
            mirror,
        )
        fold.start()
        for r in range(ROWS):
            at = 2 * d * r
            here = jnp.logical_and(lane >= at, lane < at + 2 * d)
            row = buf[C : 2 * C, columns(r)].astype(F32)
            pack = jnp.where(here, pltpu.roll(row, (at + d) % LANES, 1), pack)
        packed[e] = pack.astype(BF)
        copies = []
        for slot, target in enumerate((east, west, fold_a, fold_b)):
            copies.append(
                copy_to(
                    packed.at[e],
                    rims.at[e, slot],
                    ex_send.at[e, slot],
                    ex_recv.at[e, slot],
                    target,
                )
            )
        copies[0].start()
        copies[1].start()
        start_if(a_away, copies[2])
        start_if(b_away, copies[3])
        sends.append((None, fold))
        sends.append((None, copies[0]))
        sends.append((None, copies[1]))
        sends.append((a_away, copies[2]))
        sends.append((b_away, copies[3]))
        return copies, fold

    def receive_rims(e, buf, d, waits):
        copies, fold = waits
        copies[0].wait_recv()
        copies[1].wait_recv()
        for away, slot in ((a_away, 2), (b_away, 3)):

            @pl.when(away)
            def _():
                copies[slot].wait_recv()

            @pl.when(jnp.logical_not(away))
            def _():
                rims[e, slot] = packed[e]

        fold.wait_recv()
        low = lax.rem(lane, 2 * d) < d
        rim = [rims[e, slot].astype(F32) for slot in range(4)]
        rim = jnp.where(
            lane < 2 * d * ROWS, jnp.where(low, rim[0], rim[1]), jnp.where(low, rim[2], rim[3])
        )
        for r in range(ROWS + d):
            row = buf[C : 2 * C, columns(r)].astype(F32)
            edge = pltpu.roll(rim, (-(2 * d * r + d)) % LANES, 1)
            buf[0:C, columns(r)] = pltpu.roll(
                jnp.where(lane >= LANES - d, edge, row), d, 1
            ).astype(BF)
            buf[2 * C : 3 * C, columns(r)] = pltpu.roll(
                jnp.where(lane < d, edge, row), LANES - d, 1
            ).astype(BF)

    def all_reduce(l):
        axis_a, axis_b, axis_c = ORDERS[l]
        place_a, place_b, place_c = (coordinate(me, axis) for axis in ORDERS[l])
        half = pl.ds(pl.multiple_of(core * HALF, LANES), HALF)
        other = pl.ds(pl.multiple_of((1 - core) * HALF, LANES), HALF)
        band = pl.ds(pl.multiple_of(place_a * BAND, 16), BAND)
        count = [0]

        def post(src, dst, target):
            number = count[0]
            count[0] += 1
            copy = copy_to(src, dst, ar_send.at[l, number], ar_recv.at[l, number], target)
            copy.start()
            sends.append((None, copy))
            return copy

        def around(axis, place):
            for step in (1, 2, 3):
                to = lax.rem(place + step, 4)
                yield step - 1, to, with_coordinate(me, axis, to)

        to_mate[l] = partial[l, :, other].astype(BF)
        copy = post(to_mate.at[l], from_mate.at[l], mate)
        yield
        copy.wait_recv()
        a_out[l] = (partial[l, :, half] + from_mate[l].astype(F32)).astype(BF)
        copies = [
            post(
                a_out.at[l, pl.ds(pl.multiple_of(to * BAND, 16), BAND)], a_in.at[l, slot], target
            )
            for slot, to, target in around(axis_a, place_a)
        ]
        yield
        for copy in copies:
            copy.wait_recv()
        total = a_out[l, band].astype(F32)
        for slot in range(3):
            total = total + a_in[l, slot].astype(F32)
        b_out[l] = total.astype(BF)
        copies = [
            post(
                b_out.at[l, :, pl.ds(pl.multiple_of(to * PART, LANES), PART)],
                b_in.at[l, slot],
                target,
            )
            for slot, to, target in around(axis_b, place_b)
        ]
        yield
        for copy in copies:
            copy.wait_recv()
        total = b_out[l, :, pl.ds(pl.multiple_of(place_b * PART, LANES), PART)].astype(F32)
        for slot in range(3):
            total = total + b_in[l, slot].astype(F32)
        c_in[l, place_c] = total.astype(BF)
        copies = [
            post(c_in.at[l, place_c], c_in.at[l, place_c], target)
            for slot, to, target in around(axis_c, place_c)
        ]
        yield
        for copy in copies:
            copy.wait_recv()
        total = c_in[l, 0].astype(F32)
        for slot in range(1, 4):
            total = total + c_in[l, slot].astype(F32)
        mine = pl.ds(pl.multiple_of(core * HALF + place_b * PART, LANES), PART)
        full[l, band, mine] = total.astype(BF)
        copies = [
            post(full.at[l, band, mine], full.at[l, band, mine], target)
            for slot, to, target in around(axis_b, place_b)
        ]
        yield
        for copy in copies:
            copy.wait_recv()
        final = [post(full.at[l, band, half], full.at[l, band, half], mate)]
        copies = [
            post(full.at[l, band, half], full.at[l, band, half], target)
            for slot, to, target in around(axis_a, place_a)
        ]
        yield
        for step, copy in enumerate(copies):
            copy.wait_recv()
            source = lax.rem(place_a + 3 - step, 4)
            piece = full.at[l, pl.ds(pl.multiple_of(source * BAND, 16), BAND), half]
            final.append(post(piece, piece, mate))
        yield
        for copy in final:
            copy.wait_recv()
        dw_ref[l] = full[l]
        yield

    forward_buffers = (s0, s1, s2)
    backward_buffers = (t0, t1, t2)

    for r in range(ROWS):
        s0[C : 2 * C, columns(r)] = (x_ref[r].astype(F32) * mask).astype(BF)

    for l in range(3):
        d = 2**l
        buf = forward_buffers[l]
        waits = send_rims(l, buf, d, True)
        for a in range(3):
            for b in range(3):
                tap = w_ref[l, 3 * a + b]
                wf[l, a, :, b * C : (b + 1) * C] = tap
                wt[l, a, :, (2 - b) * C : (3 - b) * C] = tap.T
        if l > 0:
            v = slope[l - 1]
            s = jax.nn.sigmoid(v)
            slope[l - 1] = s * (1.0 + v * (1.0 - s))
        receive_rims(l, buf, d, waits)
        acc[...] = dot(wf[l, 1], buf[:, 0:CELLS]) + cols_ref[:, l : l + 1]
        acc[...] += dot(wf[l, 2], buf[:, d * LANES : CELLS + d * LANES])
        acc[:, d * LANES : CELLS] += dot(wf[l, 0], buf[:, 0 : CELLS - d * LANES])
        v = acc[...]
        slope[l] = v
        after = (
            mask * (buf[C : 2 * C, 0:CELLS].astype(F32) + v * jax.nn.sigmoid(v))
        ).astype(BF)
        if l < 2:
            forward_buffers[l + 1][C : 2 * C, 0:CELLS] = after
        else:
            for r in range(ROWS):
                out_ref[r] = after[:, columns(r)]

    v = slope[2]
    s = jax.nn.sigmoid(v)
    slope[2] = s * (1.0 + v * (1.0 - s))
    for r in range(ROWS):
        grad[:, columns(r)] = mask * ct_ref[r].astype(F32)

    running = []
    for l in (2, 1, 0):
        d = 2**l
        stored = forward_buffers[l]
        buf = backward_buffers[l]
        delta = (grad[...] * slope[l]).astype(BF)
        buf[C : 2 * C, 0:CELLS] = delta
        waits = send_rims(5 - l, buf, d, False)
        for reduction in running:
            next(reduction)
        partial[l, :, 512:640] = jnp.zeros((C, LANES), F32)
        partial[l, :, 1152:1280] = jnp.zeros((C, LANES), F32)
        partial[l, :, 1792:1920] = jnp.zeros((C, LANES), F32)
        partial[l, :, 0:576] = dot_nt(
            buf[C : 2 * C, d * LANES : CELLS], stored[:, 0 : CELLS - d * LANES]
        )
        partial[l, :, 640:1216] = dot_nt(buf[C : 2 * C, 0:CELLS], stored[:, 0:CELLS])
        partial[l, :, 1280:1856] = dot_nt(
            buf[C : 2 * C, 0:CELLS], stored[:, d * LANES : CELLS + d * LANES]
        )
        partial[l, :, 1920:2048] = jnp.broadcast_to(
            jnp.sum(buf[C : 2 * C, 0:CELLS].astype(F32), axis=1, keepdims=True), (C, LANES)
        )
        reduction = all_reduce(l)
        next(reduction)
        running.append(reduction)
        receive_rims(5 - l, buf, d, waits)
        rest = CELLS - d * LANES
        acc[...] = dot(wt[l, 1], buf[:, 0:CELLS])
        acc[:, d * LANES : CELLS] += dot(wt[l, 2], buf[:, 0:rest])
        acc[:, 0:rest] += dot(wt[l, 0], buf[:, d * LANES : CELLS])
        over = dot(wt[l, 2, :, 0:C], buf[2 * C : 3 * C, CELLS : CELLS + d * LANES])
        over += dot(wt[l, 2, :, C : 2 * C], buf[C : 2 * C, CELLS : CELLS + d * LANES])
        over += dot(wt[l, 2, :, 2 * C : 3 * C], buf[0:C, CELLS : CELLS + d * LANES])
        acc[:, rest:CELLS] += flip_sign * over
        grad[...] = mask * (grad[...] + acc[...])

    for r in range(ROWS):
        fg_ref[r] = grad[:, columns(r)].astype(BF)
    done = object()
    while running:
        running = [reduction for reduction in running if next(reduction, done) is not done]
    for condition, copy in sends:
        if condition is None:
            copy.wait_send()
        else:

            @pl.when(condition)
            def _():
                copy.wait_send()


def shards(fields, cotangent, weights, biases, ocean_tiles, velocity_mask):
    n = lax.axis_size("tiles")
    cols = jnp.concatenate(
        [
            biases.T,
            (1 - 2 * velocity_mask).astype(F32)[:, None],
            jnp.broadcast_to(ocean_tiles.astype(F32), (C, 1)),
        ],
        axis=1,
    )
    cols = jnp.pad(cols, ((0, 0), (0, LANES - cols.shape[1])))
    vmem = pl.BlockSpec(memory_space=pltpu.VMEM)
    out, field_grad, summed = pl.pallas_call(
        functools.partial(kernel, n),
        out_shape=(
            jax.ShapeDtypeStruct((ROWS, C, LANES), BF),
            jax.ShapeDtypeStruct((ROWS, C, LANES), BF),
            jax.ShapeDtypeStruct((3, C, TOTAL), BF),
        ),
        in_specs=[vmem] * 4,
        out_specs=(vmem,) * 3,
        scratch_shapes=[
            pltpu.VMEM((3 * C, CELLS + LANES), BF),
            pltpu.VMEM((3 * C, CELLS + 2 * LANES), BF),
            pltpu.VMEM((3 * C, CELLS + 4 * LANES), BF),
            pltpu.VMEM((3 * C, CELLS + LANES), BF),
            pltpu.VMEM((3 * C, CELLS + 2 * LANES), BF),
            pltpu.VMEM((3 * C, CELLS + 4 * LANES), BF),
            pltpu.VMEM((3, C, CELLS), F32),
            pltpu.VMEM((C, CELLS), F32),
            pltpu.VMEM((C, CELLS), F32),
            pltpu.VMEM((3, 3, C, 3 * C), BF),
            pltpu.VMEM((3, 3, C, 3 * C), BF),
            pltpu.VMEM((6, C, LANES), BF),
            pltpu.VMEM((6, C, 4 * LANES), BF),
            pltpu.VMEM((6, 4, C, LANES), BF),
            pltpu.VMEM((3, C, TOTAL), F32),
            pltpu.VMEM((3, C, HALF), BF),
            pltpu.VMEM((3, C, HALF), BF),
            pltpu.VMEM((3, C, HALF), BF),
            pltpu.VMEM((3, 3, BAND, HALF), BF),
            pltpu.VMEM((3, BAND, HALF), BF),
            pltpu.VMEM((3, 3, BAND, PART), BF),
            pltpu.VMEM((3, 4, BAND, PART), BF),
            pltpu.VMEM((3, C, TOTAL), BF),
            pltpu.SemaphoreType.DMA((6, 5)),
            pltpu.SemaphoreType.DMA((6, 5)),
            pltpu.SemaphoreType.DMA((3, 20)),
            pltpu.SemaphoreType.DMA((3, 20)),
        ],
        compiler_params=pltpu.CompilerParams(
            collective_id=0, has_side_effects=True, vmem_limit_bytes=56 * 1024 * 1024
        ),
        cost_estimate=pl.CostEstimate(
            flops=18 * 9 * C * C * CELLS, bytes_accessed=8 * 1024 * 1024, transcendentals=9 * C * CELLS
        ),
    )(jnp.transpose(fields, (1, 0, 2)), jnp.transpose(cotangent, (1, 0, 2)), weights, cols)
    taps = summed[:, :, : 3 * WIDE].reshape(3, C, 3, WIDE)[..., : 3 * C].reshape(3, C, 3, 3, C)
    kernel_grad = jnp.transpose(taps, (0, 2, 3, 1, 4)).reshape(3, 9, C, C).astype(F32)
    bias_grad = summed[:, :, 3 * WIDE].astype(F32)
    return (
        jnp.transpose(out, (1, 0, 2)),
        jnp.transpose(field_grad, (1, 0, 2)),
        kernel_grad,
        bias_grad,
    )


def solution(mesh):
    placed = (P(None, None, "tiles"), P(None, None, "tiles"), P(), P(), P(None, "tiles"), P())
    return jax.shard_map(
        shards,
        mesh=mesh,
        in_specs=placed,
        out_specs=(P(None, None, "tiles"), P(None, None, "tiles"), P(), P()),
        check_vma=False,
    )
```

profile of v0, /device:TPU:1, one launch (start us, length us, event | category | flops | bytes accessed | tf_op | source)
XLA Modules:
  0.0 142.3 jit_solution(2435250569501853124)
XLA Ops:
  1.3 0.1 pad.7.clone
  1.4 0.7 subtract_convert_fusion
  2.0 0.8 maximum_maximum_fusion
  2.8 0.1 copy.33
  2.9 0.7 pad.4.cols_ref
  3.6 2.1 %copy_bitcast_fusion = (bf16[8,192,128]{2,1,0:T(8,128)(2,1)}, bf16[8,192,128]{2,1,0:T(8,128)(2,1)}) fusion(bf16[192,8,128]{2,1,0:T(8,128)(2,1)} %param.7, bf16[192,8,128]{2,1,0:T(8,128)(2,1)} %param.6), kind=kLoop, calls=%fused_computation.1 | loop fusion | bytes 1572864 | tf_op jit(solution)/shard_map/transpose | solution.py:462
  5.7 106.1 %shard_map.93 = (bf16[8,192,128]{2,1,0:T(8,128)(2,1)}, bf16[8,192,128]{2,1,0:T(8,128)(2,1)}, bf16[3,192,2048]{2,1,0:T(8,128)(2,1)}) custom-call(bf16[8,192,128]{2,1,0:T(8,128)(2,1)} %get-tuple-element.27.x_ref, bf16[8,192,128]{2,1,0:T(8,128)(2,1)} %get-tuple-element.26.ct_ref, bf16[3,9,192,192]{3,2,1,0:T(8,128)(2,1)} %w_ref.1, f32[192,128]{1,0:T(8,128)} %pad.4.cols_ref), custom_call_target="tpu_custom_call" | custom-call | flops 6115295232 | bytes 8388608 | tf_op jit(solution)/shard_map/pallas_call | solution.py:418
  111.9 2.0 %copy.36 = bf16[192,8,128]{2,1,0:T(8,128)(2,1)} copy(bf16[192,8,128]{2,0,1:T(8,128)(2,1)} %bitcast.20) | data formatting | bytes 786432
  113.9 2.0 %copy.37 = bf16[192,8,128]{2,1,0:T(8,128)(2,1)} copy(bf16[192,8,128]{2,0,1:T(8,128)(2,1)} %bitcast.19) | data formatting | bytes 786432
  115.8 1.7 %convert_reduce_fusion = f32[3,192]{1,0:T(4,128)} fusion(bf16[3,192,2048]{2,1,0:T(8,128)(2,1)} %get-tuple-element.9), kind=kLoop, calls=%fused_computation.3 | loop fusion | flops 576 | bytes 3456 | tf_op jit(solution)/shard_map/convert_element_type | solution.py:465
  117.5 3.1 %slice.9 = bf16[3,192,1920]{2,1,0:T(8,128)(2,1)} slice(bf16[3,192,2048]{2,1,0:T(8,128)(2,1)} %get-tuple-element.9), slice={[0:3], [0:192], [0:1920]} | slice | bytes 4423680 | tf_op jit(solution)/shard_map/slice | solution.py:463
  120.6 5.2 %reshape.21 = bf16[3,192,3,640]{3,2,1,0:T(4,128)(2,1)S(1)} reshape(bf16[3,192,1920]{2,1,0:T(8,128)(2,1)} %slice.9) | data formatting | bytes 4423680 | tf_op jit(solution)/shard_map/reshape | solution.py:463
  125.9 2.4 %copy_convert_fusion = f32[3,192,3,576]{3,1,2,0:T(8,128)} fusion(bf16[3,192,3,576]{3,2,1,0:T(4,128)(2,1)S(1)} %bitcast.18), kind=kLoop, calls=%fused_computation | loop fusion | flops 995328 | bytes 5971968 | tf_op jit(solution)/shard_map/convert_element_type | solution.py:464
  128.3 6.9 %copy.35 = f32[3,192,3,576]{1,3,2,0:T(8,128)} copy(f32[3,192,3,576]{3,1,2,0:T(8,128)} %copy_convert_fusion) | data formatting | bytes 7962624 | tf_op jit(solution)/shard_map/convert_element_type | solution.py:464
  135.2 7.1 %copy.38 = f32[3,9,192,192]{3,2,1,0:T(8,128)} copy(f32[3,9,192,192]{2,3,1,0:T(8,128)} %bitcast.17) | data formatting | bytes 7962624
where the time goes:
time: 143 us; the launch traced here: 142 us
  Pallas kernels  106 us (74%)
  local copies, waits for them, and re-layouts  29.3 us (20%)
  other arithmetic  5.53 us (4%)
    pallas_call x1, Pallas kernels, shards(): pl.pallas_call(functools.partial(kernel, n), out_shape=(jax.ShapeDtypeStr...  106 us
    unnamed x3, local copies, waits for them, and re-layouts  11.1 us
    convert_element_type x1, local copies, waits for them, and re-layouts, shards(): jnp.transpose(taps, (0, 2, 3, 1, 4)).reshape(3, 9, C, C).astype(F32)  6.86 us
    reshape x1, local copies, waits for them, and re-layouts, shards(): summed[:, :, :3 * WIDE].reshape(3, C, 3, WIDE)[..., :3 * C]  5.23 us
    slice x1, local copies, waits for them, and re-layouts, shards(): summed[:, :, :3 * WIDE].reshape(3, C, 3, WIDE)[..., :3 * C]  3.14 us

commit v1 on v0

--- a/solution.py
+++ b/solution.py
@@ -65,7 +65,9 @@
     x_ref,
     ct_ref,
     w_ref,
-    cols_ref,
+    bias_ref,
+    ocean_ref,
+    velocity_ref,
     out_ref,
     fg_ref,
     dw_ref,
@@ -75,6 +77,8 @@
     t0,
     t1,
     t2,
+    spread_rows,
+    cols_ref,
     slope,
     acc,
     grad,
@@ -132,8 +136,13 @@
         + lax.broadcasted_iota(jnp.int32, (LANES, LANES), 1)
         == LANES - 1
     ).astype(F32).astype(BF)
-    flip_sign = cols_ref[:, 3:4]
-    mask = cols_ref[:, 4:5]
+    cols_ref[...] = jnp.zeros((LANES, 2 * LANES), F32)
+    cols_ref[0:3, 0:C] = bias_ref[...]
+    cols_ref[3:4, 0:C] = (1 - 2 * velocity_ref[...]).astype(F32).reshape(1, C)
+    turned_cols = cols_ref[...].T[0:C]
+    bias_cols = [turned_cols[:, l : l + 1] for l in range(3)]
+    flip_sign = turned_cols[:, 3:4]
+    mask = ocean_ref[0, 0].astype(F32)
     sends = []
 
     def columns(row):
@@ -314,8 +323,10 @@
     forward_buffers = (s0, s1, s2)
     backward_buffers = (t0, t1, t2)
 
+    spread_rows[...] = x_ref[...].astype(F32).reshape(C * ROWS, LANES)
     for r in range(ROWS):
-        s0[C : 2 * C, columns(r)] = (x_ref[r].astype(F32) * mask).astype(BF)
+        row = spread_rows[pl.ds(r, C, stride=ROWS), :]
+        s0[C : 2 * C, columns(r)] = (row * mask).astype(BF)
 
     for l in range(3):
         d = 2**l
@@ -331,7 +342,7 @@
             s = jax.nn.sigmoid(v)
             slope[l - 1] = s * (1.0 + v * (1.0 - s))
         receive_rims(l, buf, d, waits)
-        acc[...] = dot(wf[l, 1], buf[:, 0:CELLS]) + cols_ref[:, l : l + 1]
+        acc[...] = dot(wf[l, 1], buf[:, 0:CELLS]) + bias_cols[l]
         acc[...] += dot(wf[l, 2], buf[:, d * LANES : CELLS + d * LANES])
         acc[:, d * LANES : CELLS] += dot(wf[l, 0], buf[:, 0 : CELLS - d * LANES])
         v = acc[...]
@@ -348,8 +359,9 @@
     v = slope[2]
     s = jax.nn.sigmoid(v)
     slope[2] = s * (1.0 + v * (1.0 - s))
+    spread_rows[...] = ct_ref[...].astype(F32).reshape(C * ROWS, LANES)
     for r in range(ROWS):
-        grad[:, columns(r)] = mask * ct_ref[r].astype(F32)
+        grad[:, columns(r)] = mask * spread_rows[pl.ds(r, C, stride=ROWS), :]
 
     running = []
     for l in (2, 1, 0):
@@ -403,17 +415,25 @@
                 copy.wait_send()
 
 
+def finish(rows_a, rows_b, summed, out_a, out_b, kernel_grad, bias_grad, spread_rows, bias_rows):
+    l = pl.program_id(0)
+    for a in range(3):
+        for b in range(3):
+            first = a * WIDE + b * C
+            kernel_grad[0, 3 * a + b] = summed[0, :, first : first + C].astype(F32)
+    bias_rows[pl.ds(l, 1), :] = summed[0, :, 3 * WIDE : TOTAL].astype(F32).T[0:1]
+    bias_grad[...] = bias_rows[0:3]
+    for step, rows, out in ((0, rows_a, out_a), (1, rows_b, out_b)):
+
+        @pl.when(l == step)
+        def _():
+            for r in range(ROWS):
+                spread_rows[pl.ds(r, C, stride=ROWS), :] = rows[r].astype(F32)
+            out[...] = spread_rows[...].reshape(C, ROWS, LANES).astype(BF)
+
+
 def shards(fields, cotangent, weights, biases, ocean_tiles, velocity_mask):
     n = lax.axis_size("tiles")
-    cols = jnp.concatenate(
-        [
-            biases.T,
-            (1 - 2 * velocity_mask).astype(F32)[:, None],
-            jnp.broadcast_to(ocean_tiles.astype(F32), (C, 1)),
-        ],
-        axis=1,
-    )
-    cols = jnp.pad(cols, ((0, 0), (0, LANES - cols.shape[1])))
     vmem = pl.BlockSpec(memory_space=pltpu.VMEM)
     out, field_grad, summed = pl.pallas_call(
         functools.partial(kernel, n),
@@ -422,7 +442,7 @@
             jax.ShapeDtypeStruct((ROWS, C, LANES), BF),
             jax.ShapeDtypeStruct((3, C, TOTAL), BF),
         ),
-        in_specs=[vmem] * 4,
+        in_specs=[vmem] * 4 + [pl.BlockSpec(memory_space=pltpu.SMEM), vmem],
         out_specs=(vmem,) * 3,
         scratch_shapes=[
             pltpu.VMEM((3 * C, CELLS + LANES), BF),
@@ -431,6 +451,8 @@
             pltpu.VMEM((3 * C, CELLS + LANES), BF),
             pltpu.VMEM((3 * C, CELLS + 2 * LANES), BF),
             pltpu.VMEM((3 * C, CELLS + 4 * LANES), BF),
+            pltpu.VMEM((C * ROWS, LANES), F32),
+            pltpu.VMEM((LANES, 2 * LANES), F32),
             pltpu.VMEM((3, C, CELLS), F32),
             pltpu.VMEM((C, CELLS), F32),
             pltpu.VMEM((C, CELLS), F32),
@@ -459,16 +481,31 @@
         cost_estimate=pl.CostEstimate(
             flops=18 * 9 * C * C * CELLS, bytes_accessed=8 * 1024 * 1024, transcendentals=9 * C * CELLS
         ),
-    )(jnp.transpose(fields, (1, 0, 2)), jnp.transpose(cotangent, (1, 0, 2)), weights, cols)
-    taps = summed[:, :, : 3 * WIDE].reshape(3, C, 3, WIDE)[..., : 3 * C].reshape(3, C, 3, 3, C)
-    kernel_grad = jnp.transpose(taps, (0, 2, 3, 1, 4)).reshape(3, 9, C, C).astype(F32)
-    bias_grad = summed[:, :, 3 * WIDE].astype(F32)
-    return (
-        jnp.transpose(out, (1, 0, 2)),
-        jnp.transpose(field_grad, (1, 0, 2)),
-        kernel_grad,
-        bias_grad,
-    )
+    )(fields, cotangent, weights, biases, ocean_tiles, velocity_mask)
+    whole = lambda *shape: pl.BlockSpec(shape, lambda l: (0,) * len(shape))
+    return pl.pallas_call(
+        finish,
+        grid=(3,),
+        out_shape=(
+            jax.ShapeDtypeStruct((C, ROWS, LANES), BF),
+            jax.ShapeDtypeStruct((C, ROWS, LANES), BF),
+            jax.ShapeDtypeStruct((3, 9, C, C), F32),
+            jax.ShapeDtypeStruct((3, C), F32),
+        ),
+        in_specs=[
+            whole(ROWS, C, LANES),
+            whole(ROWS, C, LANES),
+            pl.BlockSpec((1, C, TOTAL), lambda l: (l, 0, 0)),
+        ],
+        out_specs=(
+            whole(C, ROWS, LANES),
+            whole(C, ROWS, LANES),
+            pl.BlockSpec((1, 9, C, C), lambda l: (l, 0, 0, 0)),
+            whole(3, C),
+        ),
+        scratch_shapes=[pltpu.VMEM((C * ROWS, LANES), F32), pltpu.VMEM((8, C), F32)],
+        compiler_params=pltpu.CompilerParams(vmem_limit_bytes=32 * 1024 * 1024),
+    )(out, field_grad, summed)
 
 
 def solution(mesh):

time: 143 us -> 115 us (0.80)
  local copies, waits for them, and re-layouts: 29.3 us -> 3.65 us
  other arithmetic: 5.53 us -> 0 us
  Pallas kernels: 106 us -> 110 us
    unnamed x3 -> x6, local copies, waits for them, and re-layouts: 11.1 us -> 3.65 us
    convert_element_type x1 -> x0, local copies, waits for them, and re-layouts: 6.86 us -> none  [shards(): jnp.transpose(taps, (0, 2, 3, 1, 4)).reshape(3, 9, C, C).astype(F32)]
    reshape x1 -> x0, local copies, waits for them, and re-layouts: 5.23 us -> none  [shards(): summed[:, :, :3 * WIDE].reshape(3, C, 3, WIDE)[..., :3 * C]]
    convert_element_type x3 -> x0, other arithmetic: 4.77 us -> none  [the longest x1 2.44 us: shards(): jnp.transpose(taps, (0, 2, 3, 1, 4)).reshape(3, 9, C, C).astype(F32)]
    pallas_call x0 -> x1, Pallas kernels: none -> 3.33 us  [shards(): pl.pallas_call(finish, grid=(3,), out_shape=(jax.ShapeDtypeStruct((C, ROW...]
    slice x1 -> x0, local copies, waits for them, and re-layouts: 3.14 us -> none  [shards(): summed[:, :, :3 * WIDE].reshape(3, C, 3, WIDE)[..., :3 * C]]
    transpose x1 -> x0, local copies, waits for them, and re-layouts: 2.13 us -> none  [shards(): jnp.transpose(cotangent, (1, 0, 2))]
where the time goes in v1:
time: 115 us
  Pallas kernels  110 us (96%)
  local copies, waits for them, and re-layouts  3.65 us (3%)
  between operations  1.3 us (1%)
    pallas_call x1, Pallas kernels, shards(): pl.pallas_call(functools.partial(kernel, n), out_shape=(jax.ShapeDtypeStr...  106 us
    unnamed x6, local copies, waits for them, and re-layouts  3.65 us
    pallas_call x1, Pallas kernels, shards(): pl.pallas_call(finish, grid=(3,), out_shape=(jax.ShapeDtypeStruct((C, ROW...  3.33 us

profile of v1, /device:TPU:1, one launch (start us, length us, event | category | flops | bytes accessed | tf_op | source)
XLA Modules:
  0.0 114.6 jit_solution(9100247574046728794)
XLA Ops:
  1.3 106.3 %shard_map.93 = (bf16[8,192,128]{2,1,0:T(8,128)(2,1)}, bf16[8,192,128]{2,1,0:T(8,128)(2,1)}, bf16[3,192,2048]{2,1,0:T(8,128)(2,1)}) custom-call(bf16[192,8,128]{2,1,0:T(8,128)(2,1)} %x_ref.1, bf16[192,8,128]{2,1,0:T(8,128)(2,1)} %ct_ref.1, bf16[3,9,192,192]{3,2,1,0:T(8,128)(2,1)} %w_ref.1, f32[3,192]{1,0:T(4,128)} %bias_ref.1, s32[1,1]{1,0:T(1,128)S(6)} %copy.10.ocean_ref, ...), custom_call_target="tpu_custom_call" | custom-call | flops 6115295232 | bytes 8388608 | tf_op jit(solution)/shard_map/pallas_call | solution.py:438
  107.6 0.0 copy-start
  107.6 1.7 %copy-done = bf16[3,192,2048]{2,1,0:T(8,128)(2,1)S(1)} copy-done((bf16[3,192,2048]{2,1,0:T(8,128)(2,1)S(1)}, bf16[3,192,2048]{2,1,0:T(8,128)(2,1)}, u32[]{:S(2)}) %copy-start) | copy-done | bytes 2359320
  109.3 0.0 copy-start.1
  109.3 1.0 copy-done.1
  110.3 0.0 copy-start.2
  110.3 1.0 copy-done.2
  111.3 3.3 %shard_map.94 = (bf16[192,8,128]{2,1,0:T(8,128)(2,1)}, bf16[192,8,128]{2,1,0:T(8,128)(2,1)}, f32[3,9,192,192]{3,2,1,0:T(8,128)}, f32[3,192]{1,0:T(4,128)}) custom-call(bf16[8,192,128]{2,1,0:T(8,128)(2,1)S(1)} %copy-done.1, bf16[8,192,128]{2,1,0:T(8,128)(2,1)S(1)} %copy-done.2, bf16[3,192,2048]{2,1,0:T(8,128)(2,1)S(1)} %copy-done), custom_call_target="tpu_custom_call" | custom-call | tf_op jit(solution)/shard_map/pallas_call | solution.py:486
Async XLA Ops:
  107.6 1.7 %copy-start = (bf16[3,192,2048]{2,1,0:T(8,128)(2,1)S(1)}, bf16[3,192,2048]{2,1,0:T(8,128)(2,1)}, u32[]{:S(2)}) copy-start(bf16[3,192,2048]{2,1,0:T(8,128)(2,1)} %get-tuple-element.9.summed) | copy-start | bytes 7077892
  109.3 1.0 copy-start.1
  110.3 1.0 copy-start.2

commit v2 on v1

--- a/solution.py
+++ b/solution.py
@@ -64,7 +64,7 @@
     n,
     x_ref,
     ct_ref,
-    w_ref,
+    w_hbm,
     bias_ref,
     ocean_ref,
     velocity_ref,
@@ -77,16 +77,21 @@
     t0,
     t1,
     t2,
+    w_ref,
     spread_rows,
     cols_ref,
     slope,
     acc,
     grad,
-    wf,
-    wt,
+    w_side,
+    v_mid,
+    v_side,
+    v_over,
     packed,
+    corner,
     turned,
     rims,
+    corners,
     partial,
     to_mate,
     from_mate,
@@ -96,6 +101,7 @@
     b_in,
     c_in,
     full,
+    w_sem,
     ex_send,
     ex_recv,
     ar_send,
@@ -130,6 +136,12 @@
     def _():
         pl.semaphore_signal(barrier, inc=1, device_id=(fold_b,), device_id_type=MESH)
 
+    loads = [
+        pltpu.make_async_copy(w_hbm.at[l], w_ref.at[l], w_sem.at[l]) for l in range(3)
+    ]
+    for load in loads:
+        load.start()
+
     lane = lax.broadcasted_iota(jnp.int32, (C, LANES), 1)
     flip_matrix = (
         lax.broadcasted_iota(jnp.int32, (LANES, LANES), 0)
@@ -145,90 +157,127 @@
     mask = ocean_ref[0, 0].astype(F32)
     sends = []
 
-    def columns(row):
-        return slice(row * LANES, (row + 1) * LANES)
-
-    def send_rims(e, buf, d, signed):
-        pack = jnp.zeros((C, LANES), F32)
-        for k in range(d):
-            turn = dot(buf[C : 2 * C, columns(ROWS - 1 - k)], flip_matrix)
-            if signed:
-                turn = turn * flip_sign
-            turned[e, :, columns(k)] = turn.astype(BF)
-            at = 2 * d * (ROWS + k)
-            here = jnp.logical_and(lane >= at, lane < at + 2 * d)
-            pack = jnp.where(here, pltpu.roll(turn, (at + d) % LANES, 1), pack)
-        if e == 0:
-            pl.semaphore_wait(
-                barrier,
-                len(partners) + a_away.astype(jnp.int32) + b_away.astype(jnp.int32),
+    def columns(row, count=1):
+        return slice(row * LANES, (row + count) * LANES)
+
+    class Rims:
+        def __init__(self, e, buf, d, signed):
+            self.e, self.buf, self.d, self.signed = e, buf, d, signed
+            self.folds = []
+
+        def turn(self, first, last):
+            for k in range(first, last):
+                row = dot(self.buf[0:C, columns(ROWS - 1 - k)], flip_matrix)
+                if self.signed:
+                    row = row * flip_sign
+                turned[self.e, :, columns(k)] = row.astype(BF)
+
+        def send_fold(self, first, last):
+            slot = 4 + len(self.folds)
+            fold = copy_to(
+                turned.at[self.e, :, pl.ds(first * LANES, (last - first) * LANES)],
+                self.buf.at[pl.ds(0, C), pl.ds(CELLS + first * LANES, (last - first) * LANES)],
+                ex_send.at[self.e, slot],
+                ex_recv.at[self.e, slot],
+                mirror,
             )
-
-        fold = copy_to(
-            turned.at[e, :, pl.ds(0, d * LANES)],
-            buf.at[pl.ds(C, C), pl.ds(CELLS, d * LANES)],
-            ex_send.at[e, 4],
-            ex_recv.at[e, 4],
-            mirror,
-        )
-        fold.start()
-        for r in range(ROWS):
-            at = 2 * d * r
-            here = jnp.logical_and(lane >= at, lane < at + 2 * d)
-            row = buf[C : 2 * C, columns(r)].astype(F32)
-            pack = jnp.where(here, pltpu.roll(row, (at + d) % LANES, 1), pack)
-        packed[e] = pack.astype(BF)
-        copies = []
-        for slot, target in enumerate((east, west, fold_a, fold_b)):
-            copies.append(
-                copy_to(
-                    packed.at[e],
-                    rims.at[e, slot],
-                    ex_send.at[e, slot],
-                    ex_recv.at[e, slot],
+            fold.start()
+            self.folds.append(fold)
+            sends.append((None, fold))
+
+        def pack(self, rows, count):
+            d = self.d
+            tile = jnp.zeros((C, LANES), F32)
+            for r in range(count):
+                at = 2 * d * r
+                here = jnp.logical_and(lane >= at, lane < at + 2 * d)
+                tile = jnp.where(here, pltpu.roll(rows(r).astype(F32), (at + d) % LANES, 1), tile)
+            return tile
+
+        def pack_sides(self):
+            tile = self.pack(lambda r: self.buf[0:C, columns(r)], ROWS)
+            packed[self.e] = tile.astype(BF)
+
+        def pack_corners(self):
+            tile = self.pack(lambda k: turned[self.e, :, columns(k)], self.d)
+            dense = tile[0:BAND]
+            for q in range(1, 4):
+                dense = dense + pltpu.roll(tile[q * BAND : (q + 1) * BAND], 32 * q, 1)
+            corner[self.e] = dense.astype(BF)
+
+        def send_sides(self):
+            self.sides = []
+            for slot, target in enumerate((east, west)):
+                copy = copy_to(
+                    packed.at[self.e],
+                    rims.at[self.e, slot],
+                    ex_send.at[self.e, slot],
+                    ex_recv.at[self.e, slot],
                     target,
                 )
+                copy.start()
+                self.sides.append(copy)
+                sends.append((None, copy))
+
+        def send_corners(self):
+            self.turns = []
+            for slot, target, away in ((0, fold_a, a_away), (1, fold_b, b_away)):
+                copy = copy_to(
+                    corner.at[self.e],
+                    corners.at[self.e, slot],
+                    ex_send.at[self.e, 2 + slot],
+                    ex_recv.at[self.e, 2 + slot],
+                    target,
+                )
+                start_if(away, copy)
+                self.turns.append((away, copy))
+                sends.append((away, copy))
+
+        def unpack(self, rim, row, slot):
+            buf, d = self.buf, self.d
+            center = buf[0:C, columns(row)].astype(F32)
+            edge = pltpu.roll(rim, (-(2 * d * slot + d)) % LANES, 1)
+            left = pltpu.roll(jnp.where(lane >= LANES - d, edge, center), d, 1)
+            right = pltpu.roll(jnp.where(lane < d, edge, center), LANES - d, 1)
+            buf[C : 2 * C, columns(row)] = left.astype(BF)
+            buf[2 * C : 3 * C, columns(row)] = right.astype(BF)
+
+        def receive_sides(self):
+            for copy in self.sides:
+                copy.wait_recv()
+            low = lax.rem(lane, 2 * self.d) < self.d
+            rim = jnp.where(
+                low, rims[self.e, 0].astype(F32), rims[self.e, 1].astype(F32)
             )
-        copies[0].start()
-        copies[1].start()
-        start_if(a_away, copies[2])
-        start_if(b_away, copies[3])
-        sends.append((None, fold))
-        sends.append((None, copies[0]))
-        sends.append((None, copies[1]))
-        sends.append((a_away, copies[2]))
-        sends.append((b_away, copies[3]))
-        return copies, fold
-
-    def receive_rims(e, buf, d, waits):
-        copies, fold = waits
-        copies[0].wait_recv()
-        copies[1].wait_recv()
-        for away, slot in ((a_away, 2), (b_away, 3)):
-
-            @pl.when(away)
-            def _():
-                copies[slot].wait_recv()
-
-            @pl.when(jnp.logical_not(away))
-            def _():
-                rims[e, slot] = packed[e]
-
-        fold.wait_recv()
-        low = lax.rem(lane, 2 * d) < d
-        rim = [rims[e, slot].astype(F32) for slot in range(4)]
-        rim = jnp.where(
-            lane < 2 * d * ROWS, jnp.where(low, rim[0], rim[1]), jnp.where(low, rim[2], rim[3])
-        )
-        for r in range(ROWS + d):
-            row = buf[C : 2 * C, columns(r)].astype(F32)
-            edge = pltpu.roll(rim, (-(2 * d * r + d)) % LANES, 1)
-            buf[0:C, columns(r)] = pltpu.roll(
-                jnp.where(lane >= LANES - d, edge, row), d, 1
-            ).astype(BF)
-            buf[2 * C : 3 * C, columns(r)] = pltpu.roll(
-                jnp.where(lane < d, edge, row), LANES - d, 1
-            ).astype(BF)
+            for r in range(ROWS):
+                self.unpack(rim, r, r)
+
+        def receive_fold(self):
+            for slot, (away, copy) in enumerate(self.turns):
+
+                @pl.when(away)
+                def _():
+                    copy.wait_recv()
+
+                @pl.when(jnp.logical_not(away))
+                def _():
+                    corners[self.e, slot] = corner[self.e]
+
+            for fold in self.folds:
+                fold.wait_recv()
+            low = lax.rem(lane, 2 * self.d) < self.d
+            tiles = []
+            for slot in range(2):
+                dense = corners[self.e, slot].astype(F32)
+                tiles.append(
+                    jnp.concatenate(
+                        [dense] + [pltpu.roll(dense, LANES - 32 * q, 1) for q in range(1, 4)],
+                        axis=0,
+                    )
+                )
+            rim = jnp.where(low, tiles[0], tiles[1])
+            for k in range(self.d):
+                self.unpack(rim, ROWS + k, k)
 
     def all_reduce(l):
         axis_a, axis_b, axis_c = ORDERS[l]
@@ -303,11 +352,11 @@
         yield
         for copy in copies:
             copy.wait_recv()
-        final = [post(full.at[l, band, half], full.at[l, band, half], mate)]
         copies = [
             post(full.at[l, band, half], full.at[l, band, half], target)
             for slot, to, target in around(axis_a, place_a)
         ]
+        final = [post(full.at[l, band, half], full.at[l, band, half], mate)]
         yield
         for step, copy in enumerate(copies):
             copy.wait_recv()
@@ -320,88 +369,150 @@
         dw_ref[l] = full[l]
         yield
 
+    def prepare_forward(l):
+        for a in range(3):
+            w_side[l, a, :, 0:C] = w_ref[l, 3 * a]
+            w_side[l, a, :, C : 2 * C] = w_ref[l, 3 * a + 2]
+
+    def prepare_backward(l):
+        for a in range(3):
+            v_mid[l, a] = w_ref[l, 3 * a + 1].T
+            v_side[l, a, :, 0:C] = w_ref[l, 3 * a + 2].T
+            v_side[l, a, :, C : 2 * C] = w_ref[l, 3 * a].T
+        for place, tap in enumerate((7, 6, 8)):
+            v_over[l, :, place * C : (place + 1) * C] = (
+                w_ref[l, tap].T.astype(F32) * flip_sign
+            ).astype(BF)
+
     forward_buffers = (s0, s1, s2)
     backward_buffers = (t0, t1, t2)
 
     spread_rows[...] = x_ref[...].astype(F32).reshape(C * ROWS, LANES)
     for r in range(ROWS):
         row = spread_rows[pl.ds(r, C, stride=ROWS), :]
-        s0[C : 2 * C, columns(r)] = (row * mask).astype(BF)
-
-    for l in range(3):
-        d = 2**l
-        buf = forward_buffers[l]
-        waits = send_rims(l, buf, d, True)
-        for a in range(3):
-            for b in range(3):
-                tap = w_ref[l, 3 * a + b]
-                wf[l, a, :, b * C : (b + 1) * C] = tap
-                wt[l, a, :, (2 - b) * C : (3 - b) * C] = tap.T
-        if l > 0:
-            v = slope[l - 1]
-            s = jax.nn.sigmoid(v)
-            slope[l - 1] = s * (1.0 + v * (1.0 - s))
-        receive_rims(l, buf, d, waits)
-        acc[...] = dot(wf[l, 1], buf[:, 0:CELLS]) + bias_cols[l]
-        acc[...] += dot(wf[l, 2], buf[:, d * LANES : CELLS + d * LANES])
-        acc[:, d * LANES : CELLS] += dot(wf[l, 0], buf[:, 0 : CELLS - d * LANES])
-        v = acc[...]
-        slope[l] = v
-        after = (
-            mask * (buf[C : 2 * C, 0:CELLS].astype(F32) + v * jax.nn.sigmoid(v))
-        ).astype(BF)
-        if l < 2:
-            forward_buffers[l + 1][C : 2 * C, 0:CELLS] = after
-        else:
-            for r in range(ROWS):
-                out_ref[r] = after[:, columns(r)]
-
-    v = slope[2]
-    s = jax.nn.sigmoid(v)
-    slope[2] = s * (1.0 + v * (1.0 - s))
+        s0[0:C, columns(r)] = (row * mask).astype(BF)
+    rim = Rims(0, s0, 1, True)
+    rim.turn(0, 1)
+    rim.pack_sides()
+    rim.pack_corners()
+    loads[0].wait()
+    prepare_forward(0)
     spread_rows[...] = ct_ref[...].astype(F32).reshape(C * ROWS, LANES)
     for r in range(ROWS):
         grad[:, columns(r)] = mask * spread_rows[pl.ds(r, C, stride=ROWS), :]
+    loads[1].wait()
+    loads[2].wait()
+    pl.semaphore_wait(
+        barrier, len(partners) + a_away.astype(jnp.int32) + b_away.astype(jnp.int32)
+    )
+    rim.send_fold(0, 1)
+    rim.send_corners()
+    rim.send_sides()
+
+    for l in range(3):
+        d = 2**l
+        rest = CELLS - d * LANES
+        buf = forward_buffers[l]
+        acc[...] = dot(w_ref[l, 4], buf[0:C, 0:CELLS]) + bias_cols[l]
+        acc[:, 0:rest] += dot(w_ref[l, 7], buf[0:C, d * LANES : CELLS])
+        acc[:, d * LANES : CELLS] += dot(w_ref[l, 1], buf[0:C, 0:rest])
+        if l < 2:
+            prepare_forward(l + 1)
+        prepare_backward(2 - l)
+        rim.receive_sides()
+        acc[...] += dot(w_side[l, 1], buf[C : 3 * C, 0:CELLS])
+        acc[:, 0:rest] += dot(w_side[l, 2], buf[C : 3 * C, d * LANES : CELLS])
+        acc[:, d * LANES : CELLS] += dot(w_side[l, 0], buf[C : 3 * C, 0:rest])
+
+        def activate(first, last):
+            v = acc[:, first:last]
+            s = jax.nn.sigmoid(v)
+            after = mask * (buf[0:C, first:last].astype(F32) + v * s)
+            s = s * (1.0 + v * (1.0 - s))
+            slope[l, :, first:last] = s
+            if l < 2:
+                forward_buffers[l + 1][0:C, first:last] = after.astype(BF)
+            else:
+                for r in range(first // LANES, last // LANES):
+                    out_ref[r] = after[:, r * LANES - first : (r + 1) * LANES - first].astype(BF)
+                t2[0:C, first:last] = (grad[:, first:last] * s).astype(BF)
+
+        activate(0, rest)
+        if l < 2:
+            later = Rims(l + 1, forward_buffers[l + 1], 2 * d, True)
+            later.turn(d, 2 * d)
+            later.send_fold(d, 2 * d)
+        else:
+            later = Rims(3, t2, d, False)
+        rim.receive_fold()
+        acc[:, rest:CELLS] += dot(w_ref[l, 7], buf[0:C, CELLS : CELLS + d * LANES]) + dot(
+            w_side[l, 2], buf[C : 3 * C, CELLS : CELLS + d * LANES]
+        )
+        activate(rest, CELLS)
+        rim = later
+        rim.turn(0, d)
+        rim.send_fold(0, d)
+        rim.pack_corners()
+        rim.send_corners()
+        rim.pack_sides()
+        rim.send_sides()
 
     running = []
     for l in (2, 1, 0):
         d = 2**l
+        rest = CELLS - d * LANES
         stored = forward_buffers[l]
         buf = backward_buffers[l]
-        delta = (grad[...] * slope[l]).astype(BF)
-        buf[C : 2 * C, 0:CELLS] = delta
-        waits = send_rims(5 - l, buf, d, False)
         for reduction in running:
             next(reduction)
         partial[l, :, 512:640] = jnp.zeros((C, LANES), F32)
         partial[l, :, 1152:1280] = jnp.zeros((C, LANES), F32)
         partial[l, :, 1792:1920] = jnp.zeros((C, LANES), F32)
-        partial[l, :, 0:576] = dot_nt(
-            buf[C : 2 * C, d * LANES : CELLS], stored[:, 0 : CELLS - d * LANES]
-        )
-        partial[l, :, 640:1216] = dot_nt(buf[C : 2 * C, 0:CELLS], stored[:, 0:CELLS])
+        partial[l, :, 0:576] = dot_nt(buf[0:C, d * LANES : CELLS], stored[:, 0:rest])
+        partial[l, :, 640:1216] = dot_nt(buf[0:C, 0:CELLS], stored[:, 0:CELLS])
         partial[l, :, 1280:1856] = dot_nt(
-            buf[C : 2 * C, 0:CELLS], stored[:, d * LANES : CELLS + d * LANES]
+            buf[0:C, 0:CELLS], stored[:, d * LANES : CELLS + d * LANES]
         )
         partial[l, :, 1920:2048] = jnp.broadcast_to(
-            jnp.sum(buf[C : 2 * C, 0:CELLS].astype(F32), axis=1, keepdims=True), (C, LANES)
+            jnp.sum(buf[0:C, 0:CELLS].astype(F32), axis=1, keepdims=True), (C, LANES)
         )
         reduction = all_reduce(l)
         next(reduction)
         running.append(reduction)
-        receive_rims(5 - l, buf, d, waits)
-        rest = CELLS - d * LANES
-        acc[...] = dot(wt[l, 1], buf[:, 0:CELLS])
-        acc[:, d * LANES : CELLS] += dot(wt[l, 2], buf[:, 0:rest])
-        acc[:, 0:rest] += dot(wt[l, 0], buf[:, d * LANES : CELLS])
-        over = dot(wt[l, 2, :, 0:C], buf[2 * C : 3 * C, CELLS : CELLS + d * LANES])
-        over += dot(wt[l, 2, :, C : 2 * C], buf[C : 2 * C, CELLS : CELLS + d * LANES])
-        over += dot(wt[l, 2, :, 2 * C : 3 * C], buf[0:C, CELLS : CELLS + d * LANES])
-        acc[:, rest:CELLS] += flip_sign * over
-        grad[...] = mask * (grad[...] + acc[...])
-
-    for r in range(ROWS):
-        fg_ref[r] = grad[:, columns(r)].astype(BF)
+        acc[...] = dot(v_mid[l, 1], buf[0:C, 0:CELLS])
+        acc[:, d * LANES : CELLS] += dot(v_mid[l, 2], buf[0:C, 0:rest])
+        acc[:, 0:rest] += dot(v_mid[l, 0], buf[0:C, d * LANES : CELLS])
+        rim.receive_sides()
+        acc[...] += dot(v_side[l, 1], buf[C : 3 * C, 0:CELLS])
+        acc[:, d * LANES : CELLS] += dot(v_side[l, 2], buf[C : 3 * C, 0:rest])
+        acc[:, 0:rest] += dot(v_side[l, 0], buf[C : 3 * C, d * LANES : CELLS])
+
+        def descend(first, last):
+            g = mask * (grad[:, first:last] + acc[:, first:last])
+            if l > 0:
+                grad[:, first:last] = g
+                backward_buffers[l - 1][0:C, first:last] = (
+                    g * slope[l - 1, :, first:last]
+                ).astype(BF)
+            else:
+                for r in range(first // LANES, last // LANES):
+                    fg_ref[r] = g[:, r * LANES - first : (r + 1) * LANES - first].astype(BF)
+
+        descend(0, rest)
+        for reduction in running:
+            next(reduction)
+        rim.receive_fold()
+        acc[:, rest:CELLS] += dot(v_over[l], buf[:, CELLS : CELLS + d * LANES])
+        descend(rest, CELLS)
+        if l > 0:
+            rim = Rims(6 - l, backward_buffers[l - 1], d // 2, False)
+            rim.turn(0, d // 2)
+            rim.send_fold(0, d // 2)
+            rim.pack_corners()
+            rim.send_corners()
+            rim.pack_sides()
+            rim.send_sides()
+
     done = object()
     while running:
         running = [reduction for reduction in running if next(reduction, done) is not done]
@@ -419,7 +530,7 @@
     l = pl.program_id(0)
     for a in range(3):
         for b in range(3):
-            first = a * WIDE + b * C
+            first = a * WIDE + (1, 0, 2)[b] * C
             kernel_grad[0, 3 * a + b] = summed[0, :, first : first + C].astype(F32)
     bias_rows[pl.ds(l, 1), :] = summed[0, :, 3 * WIDE : TOTAL].astype(F32).T[0:1]
     bias_grad[...] = bias_rows[0:3]
@@ -442,7 +553,14 @@
             jax.ShapeDtypeStruct((ROWS, C, LANES), BF),
             jax.ShapeDtypeStruct((3, C, TOTAL), BF),
         ),
-        in_specs=[vmem] * 4 + [pl.BlockSpec(memory_space=pltpu.SMEM), vmem],
+        in_specs=[
+            vmem,
+            vmem,
+            pl.BlockSpec(memory_space=pl.ANY),
+            vmem,
+            pl.BlockSpec(memory_space=pltpu.SMEM),
+            vmem,
+        ],
         out_specs=(vmem,) * 3,
         scratch_shapes=[
             pltpu.VMEM((3 * C, CELLS + LANES), BF),
@@ -451,16 +569,21 @@
             pltpu.VMEM((3 * C, CELLS + LANES), BF),
             pltpu.VMEM((3 * C, CELLS + 2 * LANES), BF),
             pltpu.VMEM((3 * C, CELLS + 4 * LANES), BF),
+            pltpu.VMEM((3, 9, C, C), BF),
             pltpu.VMEM((C * ROWS, LANES), F32),
             pltpu.VMEM((LANES, 2 * LANES), F32),
             pltpu.VMEM((3, C, CELLS), F32),
             pltpu.VMEM((C, CELLS), F32),
             pltpu.VMEM((C, CELLS), F32),
-            pltpu.VMEM((3, 3, C, 3 * C), BF),
-            pltpu.VMEM((3, 3, C, 3 * C), BF),
+            pltpu.VMEM((3, 3, C, 2 * C), BF),
+            pltpu.VMEM((3, 3, C, C), BF),
+            pltpu.VMEM((3, 3, C, 2 * C), BF),
+            pltpu.VMEM((3, C, 3 * C), BF),
             pltpu.VMEM((6, C, LANES), BF),
+            pltpu.VMEM((6, BAND, LANES), BF),
             pltpu.VMEM((6, C, 4 * LANES), BF),
-            pltpu.VMEM((6, 4, C, LANES), BF),
+            pltpu.VMEM((6, 2, C, LANES), BF),
+            pltpu.VMEM((6, 2, BAND, LANES), BF),
             pltpu.VMEM((3, C, TOTAL), F32),
             pltpu.VMEM((3, C, HALF), BF),
             pltpu.VMEM((3, C, HALF), BF),
@@ -470,13 +593,14 @@
             pltpu.VMEM((3, 3, BAND, PART), BF),
             pltpu.VMEM((3, 4, BAND, PART), BF),
             pltpu.VMEM((3, C, TOTAL), BF),
-            pltpu.SemaphoreType.DMA((6, 5)),
-            pltpu.SemaphoreType.DMA((6, 5)),
+            pltpu.SemaphoreType.DMA((3,)),
+            pltpu.SemaphoreType.DMA((6, 6)),
+            pltpu.SemaphoreType.DMA((6, 6)),
             pltpu.SemaphoreType.DMA((3, 20)),
             pltpu.SemaphoreType.DMA((3, 20)),
         ],
         compiler_params=pltpu.CompilerParams(
-            collective_id=0, has_side_effects=True, vmem_limit_bytes=56 * 1024 * 1024
+            collective_id=0, has_side_effects=True, vmem_limit_bytes=48 * 1024 * 1024
         ),
         cost_estimate=pl.CostEstimate(
             flops=18 * 9 * C * C * CELLS, bytes_accessed=8 * 1024 * 1024, transcendentals=9 * C * CELLS

time: 115 us -> 105 us (0.913)
  Pallas kernels: 110 us -> 100 us
    pallas_call x1, Pallas kernels: 106 us -> 96.9 us  [shards(): pl.pallas_call(functools.partial(kernel, n), out_shape=(jax.ShapeDtypeStr...]
    unnamed x6 -> x8, local copies, waits for them, and re-layouts: 3.65 us -> 3.35 us
where the time goes in v2:
time: 105 us
  Pallas kernels  100 us (95%)
  local copies, waits for them, and re-layouts  3.35 us (3%)
  between operations  1.3 us (1%)
    pallas_call x1, Pallas kernels, shards(): pl.pallas_call(functools.partial(kernel, n), out_shape=(jax.ShapeDtypeStr...  96.9 us
    pallas_call x1, Pallas kernels, shards(): pl.pallas_call(finish, grid=(3,), out_shape=(jax.ShapeDtypeStruct((C, ROW...  3.36 us
    unnamed x8, local copies, waits for them, and re-layouts  3.35 us

profile of v2, /device:TPU:1, one launch (start us, length us, event | category | flops | bytes accessed | tf_op | source)
XLA Modules:
  0.0 104.9 jit_solution(11561024946407261553)
XLA Ops:
  1.3 0.0 copy-start
  1.3 1.0 copy-done
  2.3 0.0 copy-start.1
  2.3 1.0 copy-done.1
  3.3 0.0 copy-start.2
  3.3 0.7 copy-done.2
  4.0 0.0 copy-start.3
  4.0 0.7 copy-done.3
  4.6 96.9 %shard_map.93 = (bf16[8,192,128]{2,1,0:T(8,128)(2,1)S(1)}, bf16[8,192,128]{2,1,0:T(8,128)(2,1)S(1)}, bf16[3,192,2048]{2,1,0:T(8,128)(2,1)S(1)}) custom-call(bf16[192,8,128]{2,1,0:T(8,128)(2,1)S(1)} %copy-done, bf16[192,8,128]{2,1,0:T(8,128)(2,1)S(1)} %copy-done.1, bf16[3,9,192,192]{3,2,1,0:T(8,128)(2,1)} %w_hbm.1, f32[3,192]{1,0:T(4,128)S(1)} %copy-done.2, ...), custom_call_target="tpu_custom_call" | custom-call | flops 6115295232 | bytes 8388608 | tf_op jit(solution)/shard_map/pallas_call | solution.py:549
  101.6 3.4 %shard_map.94 = (bf16[192,8,128]{2,1,0:T(8,128)(2,1)}, bf16[192,8,128]{2,1,0:T(8,128)(2,1)}, f32[3,9,192,192]{3,2,1,0:T(8,128)}, f32[3,192]{1,0:T(4,128)}) custom-call(bf16[8,192,128]{2,1,0:T(8,128)(2,1)S(1)} %get-tuple-element.7.rows_a, bf16[8,192,128]{2,1,0:T(8,128)(2,1)S(1)} %get-tuple-element.8.rows_b, bf16[3,192,2048]{2,1,0:T(8,128)(2,1)S(1)} %get-tuple-element.9.summed), custom_call_target="tpu_custom_call" | custom-call | tf_op jit(solution)/shard_map/pallas_call | solution.py:610
Async XLA Ops:
  1.3 1.0 copy-start
  2.3 1.0 copy-start.1
  3.3 0.7 copy-start.2
  4.0 0.7 copy-start.3

commit v3 on v2

--- a/solution.py
+++ b/solution.py
@@ -15,7 +15,6 @@
 TOTAL = 2048
 HALF = TOTAL // 2
 BAND = C // 4
-PART = HALF // 4
 BF = jnp.bfloat16
 F32 = jnp.float32
 MESH = pl.DeviceIdType.MESH
@@ -24,7 +23,11 @@
 Y = (2, 4)
 X = (8, 4)
 Z = (32, 4)
-ORDERS = ((Y, X, Z), (Z, Y, X), (X, Z, Y))
+PARTS = (
+    (pl.ds(0, 384), (Y, X, Z)),
+    (pl.ds(384, 384), (Z, Y, X)),
+    (pl.ds(768, 256), (X, Z, Y)),
+)
 
 
 def coordinate(me, axis):
@@ -62,22 +65,28 @@
 
 def kernel(
     n,
-    x_ref,
-    ct_ref,
+    x_hbm,
+    ct_hbm,
     w_hbm,
-    bias_ref,
+    bias_hbm,
     ocean_ref,
-    velocity_ref,
-    out_ref,
-    fg_ref,
-    dw_ref,
+    velocity_hbm,
+    out_hbm,
+    fg_hbm,
+    dw_hbm,
     s0,
     s1,
     s2,
     t0,
     t1,
     t2,
+    x_ref,
+    ct_ref,
+    bias_ref,
+    velocity_ref,
     w_ref,
+    out_ref,
+    fg_ref,
     spread_rows,
     cols_ref,
     slope,
@@ -97,11 +106,11 @@
     from_mate,
     a_out,
     a_in,
-    b_out,
     b_in,
     c_in,
     full,
     w_sem,
+    out_sem,
     ex_send,
     ex_recv,
     ar_send,
@@ -136,10 +145,21 @@
     def _():
         pl.semaphore_signal(barrier, inc=1, device_id=(fold_b,), device_id_type=MESH)
 
+    small = [
+        pltpu.make_async_copy(src, dst, w_sem.at[3 + number])
+        for number, (src, dst) in enumerate(
+            (
+                (bias_hbm, bias_ref),
+                (velocity_hbm, velocity_ref),
+                (x_hbm, x_ref),
+                (ct_hbm, ct_ref),
+            )
+        )
+    ]
     loads = [
         pltpu.make_async_copy(w_hbm.at[l], w_ref.at[l], w_sem.at[l]) for l in range(3)
     ]
-    for load in loads:
+    for load in small + loads:
         load.start()
 
     lane = lax.broadcasted_iota(jnp.int32, (C, LANES), 1)
@@ -149,6 +169,8 @@
         == LANES - 1
     ).astype(F32).astype(BF)
     cols_ref[...] = jnp.zeros((LANES, 2 * LANES), F32)
+    small[0].wait()
+    small[1].wait()
     cols_ref[0:3, 0:C] = bias_ref[...]
     cols_ref[3:4, 0:C] = (1 - 2 * velocity_ref[...]).astype(F32).reshape(1, C)
     turned_cols = cols_ref[...].T[0:C]
@@ -156,6 +178,13 @@
     flip_sign = turned_cols[:, 3:4]
     mask = ocean_ref[0, 0].astype(F32)
     sends = []
+
+    stores = []
+
+    def store(src, dst):
+        copy = pltpu.make_async_copy(src, dst, out_sem.at[len(stores)])
+        copy.start()
+        stores.append(copy)
 
     def columns(row, count=1):
         return slice(row * LANES, (row + count) * LANES)
@@ -182,7 +211,7 @@
                 mirror,
             )
             fold.start()
-            self.folds.append(fold)
+            self.folds.append((fold, first, last))
             sends.append((None, fold))
 
         def pack(self, rows, count):
@@ -252,7 +281,7 @@
             for r in range(ROWS):
                 self.unpack(rim, r, r)
 
-        def receive_fold(self):
+        def receive_corners(self):
             for slot, (away, copy) in enumerate(self.turns):
 
                 @pl.when(away)
@@ -263,8 +292,6 @@
                 def _():
                     corners[self.e, slot] = corner[self.e]
 
-            for fold in self.folds:
-                fold.wait_recv()
             low = lax.rem(lane, 2 * self.d) < self.d
             tiles = []
             for slot in range(2):
@@ -275,16 +302,17 @@
                         axis=0,
                     )
                 )
-            rim = jnp.where(low, tiles[0], tiles[1])
-            for k in range(self.d):
-                self.unpack(rim, ROWS + k, k)
+            self.rim = jnp.where(low, tiles[0], tiles[1])
+
+        def receive_fold(self, number):
+            fold, first, last = self.folds[number]
+            fold.wait_recv()
+            for k in range(first, last):
+                self.unpack(self.rim, ROWS + k, k)
 
     def all_reduce(l):
-        axis_a, axis_b, axis_c = ORDERS[l]
-        place_a, place_b, place_c = (coordinate(me, axis) for axis in ORDERS[l])
         half = pl.ds(pl.multiple_of(core * HALF, LANES), HALF)
         other = pl.ds(pl.multiple_of((1 - core) * HALF, LANES), HALF)
-        band = pl.ds(pl.multiple_of(place_a * BAND, 16), BAND)
         count = [0]
 
         def post(src, dst, target):
@@ -295,78 +323,75 @@
             sends.append((None, copy))
             return copy
 
-        def around(axis, place):
+        def around(axis):
             for step in (1, 2, 3):
-                to = lax.rem(place + step, 4)
+                to = lax.rem(coordinate(me, axis) + step, 4)
                 yield step - 1, to, with_coordinate(me, axis, to)
+
+        def exchange(total, landing, axis, lanes):
+            mine = coordinate(me, axis)
+            landing[mine, :, lanes] = total.astype(BF)
+            piece = landing.at[mine, :, lanes]
+            return [post(piece, piece, target) for slot, to, target in around(axis)]
+
+        def arrived(landing, copies, lanes):
+            for copy in copies:
+                copy.wait_recv()
+            total = landing[0, :, lanes].astype(F32)
+            for slot in range(1, 4):
+                total = total + landing[slot, :, lanes].astype(F32)
+            return total
 
         to_mate[l] = partial[l, :, other].astype(BF)
         copy = post(to_mate.at[l], from_mate.at[l], mate)
         yield
         copy.wait_recv()
         a_out[l] = (partial[l, :, half] + from_mate[l].astype(F32)).astype(BF)
-        copies = [
-            post(
-                a_out.at[l, pl.ds(pl.multiple_of(to * BAND, 16), BAND)], a_in.at[l, slot], target
+        waits = []
+        for lanes, axes in PARTS:
+            waits.append(
+                [
+                    post(
+                        a_out.at[l, pl.ds(pl.multiple_of(to * BAND, 16), BAND), lanes],
+                        a_in.at[l, slot, :, lanes],
+                        target,
+                    )
+                    for slot, to, target in around(axes[0])
+                ]
             )
-            for slot, to, target in around(axis_a, place_a)
-        ]
         yield
-        for copy in copies:
-            copy.wait_recv()
-        total = a_out[l, band].astype(F32)
-        for slot in range(3):
-            total = total + a_in[l, slot].astype(F32)
-        b_out[l] = total.astype(BF)
-        copies = [
-            post(
-                b_out.at[l, :, pl.ds(pl.multiple_of(to * PART, LANES), PART)],
-                b_in.at[l, slot],
-                target,
-            )
-            for slot, to, target in around(axis_b, place_b)
-        ]
+        for part, (lanes, axes) in enumerate(PARTS):
+            for copy in waits[part]:
+                copy.wait_recv()
+            band = pl.ds(pl.multiple_of(coordinate(me, axes[0]) * BAND, 16), BAND)
+            total = a_out[l, band, lanes].astype(F32)
+            for slot in range(3):
+                total = total + a_in[l, slot, :, lanes].astype(F32)
+            waits[part] = exchange(total, b_in.at[l], axes[1], lanes)
         yield
-        for copy in copies:
-            copy.wait_recv()
-        total = b_out[l, :, pl.ds(pl.multiple_of(place_b * PART, LANES), PART)].astype(F32)
-        for slot in range(3):
-            total = total + b_in[l, slot].astype(F32)
-        c_in[l, place_c] = total.astype(BF)
-        copies = [
-            post(c_in.at[l, place_c], c_in.at[l, place_c], target)
-            for slot, to, target in around(axis_c, place_c)
-        ]
+        for part, (lanes, axes) in enumerate(PARTS):
+            total = arrived(b_in.at[l], waits[part], lanes)
+            waits[part] = exchange(total, c_in.at[l], axes[2], lanes)
         yield
-        for copy in copies:
-            copy.wait_recv()
-        total = c_in[l, 0].astype(F32)
-        for slot in range(1, 4):
-            total = total + c_in[l, slot].astype(F32)
-        mine = pl.ds(pl.multiple_of(core * HALF + place_b * PART, LANES), PART)
-        full[l, band, mine] = total.astype(BF)
-        copies = [
-            post(full.at[l, band, mine], full.at[l, band, mine], target)
-            for slot, to, target in around(axis_b, place_b)
-        ]
+        for part, (lanes, axes) in enumerate(PARTS):
+            total = arrived(c_in.at[l], waits[part], lanes)
+            band = pl.ds(pl.multiple_of(coordinate(me, axes[0]) * BAND, 16), BAND)
+            here = pl.ds(pl.multiple_of(core * HALF + lanes.start, LANES), lanes.size)
+            full[l, band, here] = total.astype(BF)
+            piece = full.at[l, band, here]
+            waits[part] = [post(piece, piece, target) for slot, to, target in around(axes[0])]
         yield
-        for copy in copies:
-            copy.wait_recv()
-        copies = [
-            post(full.at[l, band, half], full.at[l, band, half], target)
-            for slot, to, target in around(axis_a, place_a)
-        ]
-        final = [post(full.at[l, band, half], full.at[l, band, half], mate)]
-        yield
-        for step, copy in enumerate(copies):
-            copy.wait_recv()
-            source = lax.rem(place_a + 3 - step, 4)
-            piece = full.at[l, pl.ds(pl.multiple_of(source * BAND, 16), BAND), half]
+        final = []
+        for part, (lanes, axes) in enumerate(PARTS):
+            for copy in waits[part]:
+                copy.wait_recv()
+            here = pl.ds(pl.multiple_of(core * HALF + lanes.start, LANES), lanes.size)
+            piece = full.at[l, :, here]
             final.append(post(piece, piece, mate))
         yield
         for copy in final:
             copy.wait_recv()
-        dw_ref[l] = full[l]
+        store(full.at[l], dw_hbm.at[l])
         yield
 
     def prepare_forward(l):
@@ -387,6 +412,7 @@
     forward_buffers = (s0, s1, s2)
     backward_buffers = (t0, t1, t2)
 
+    small[2].wait()
     spread_rows[...] = x_ref[...].astype(F32).reshape(C * ROWS, LANES)
     for r in range(ROWS):
         row = spread_rows[pl.ds(r, C, stride=ROWS), :]
@@ -397,6 +423,7 @@
     rim.pack_corners()
     loads[0].wait()
     prepare_forward(0)
+    small[3].wait()
     spread_rows[...] = ct_ref[...].astype(F32).reshape(C * ROWS, LANES)
     for r in range(ROWS):
         grad[:, columns(r)] = mask * spread_rows[pl.ds(r, C, stride=ROWS), :]
@@ -405,8 +432,8 @@
     pl.semaphore_wait(
         barrier, len(partners) + a_away.astype(jnp.int32) + b_away.astype(jnp.int32)
     )
+    rim.send_corners()
     rim.send_fold(0, 1)
-    rim.send_corners()
     rim.send_sides()
 
     for l in range(3):
@@ -444,19 +471,26 @@
             later.send_fold(d, 2 * d)
         else:
             later = Rims(3, t2, d, False)
-        rim.receive_fold()
+        rim.receive_corners()
+        for number in range(len(rim.folds)):
+            rim.receive_fold(number)
         acc[:, rest:CELLS] += dot(w_ref[l, 7], buf[0:C, CELLS : CELLS + d * LANES]) + dot(
             w_side[l, 2], buf[C : 3 * C, CELLS : CELLS + d * LANES]
         )
         activate(rest, CELLS)
         rim = later
         rim.turn(0, d)
-        rim.send_fold(0, d)
         rim.pack_corners()
         rim.send_corners()
+        if l < 2:
+            rim.send_fold(0, d)
+        else:
+            rim.send_fold(d // 2, d)
+            rim.send_fold(0, d // 2)
         rim.pack_sides()
         rim.send_sides()
 
+    store(out_ref, out_hbm)
     running = []
     for l in (2, 1, 0):
         d = 2**l
@@ -501,18 +535,31 @@
         descend(0, rest)
         for reduction in running:
             next(reduction)
-        rim.receive_fold()
-        acc[:, rest:CELLS] += dot(v_over[l], buf[:, CELLS : CELLS + d * LANES])
-        descend(rest, CELLS)
+        rim.receive_corners()
+        middle = d // 2
+        for number, (fold, first, last) in enumerate(rim.folds):
+            rim.receive_fold(number)
+            top = slice(rest + first * LANES, rest + last * LANES)
+            acc[:, top] += dot(
+                v_over[l], buf[:, CELLS + first * LANES : CELLS + last * LANES]
+            )
+            descend(top.start, top.stop)
+            if l > 0 and number == 0:
+                later = Rims(6 - l, backward_buffers[l - 1], middle, False)
+                later.turn(0, middle)
+                later.pack_corners()
+                later.send_corners()
+                if middle > 1:
+                    later.send_fold(middle // 2, middle)
+                    later.send_fold(0, middle // 2)
+                else:
+                    later.send_fold(0, 1)
         if l > 0:
-            rim = Rims(6 - l, backward_buffers[l - 1], d // 2, False)
-            rim.turn(0, d // 2)
-            rim.send_fold(0, d // 2)
-            rim.pack_corners()
-            rim.send_corners()
+            rim = later
             rim.pack_sides()
             rim.send_sides()
 
+    store(fg_ref, fg_hbm)
     done = object()
     while running:
         running = [reduction for reduction in running if next(reduction, done) is not done]
@@ -524,6 +571,9 @@
             @pl.when(condition)
             def _():
                 copy.wait_send()
+
+    for copy in stores:
+        copy.wait()
 
 
 def finish(rows_a, rows_b, summed, out_a, out_b, kernel_grad, bias_grad, spread_rows, bias_rows):
@@ -545,7 +595,7 @@
 
 def shards(fields, cotangent, weights, biases, ocean_tiles, velocity_mask):
     n = lax.axis_size("tiles")
-    vmem = pl.BlockSpec(memory_space=pltpu.VMEM)
+    hbm = pl.BlockSpec(memory_space=pltpu.HBM)
     out, field_grad, summed = pl.pallas_call(
         functools.partial(kernel, n),
         out_shape=(
@@ -554,14 +604,14 @@
             jax.ShapeDtypeStruct((3, C, TOTAL), BF),
         ),
         in_specs=[
-            vmem,
-            vmem,
-            pl.BlockSpec(memory_space=pl.ANY),
-            vmem,
+            hbm,
+            hbm,
+            hbm,
+            hbm,
             pl.BlockSpec(memory_space=pltpu.SMEM),
-            vmem,
+            hbm,
         ],
-        out_specs=(vmem,) * 3,
+        out_specs=(hbm,) * 3,
         scratch_shapes=[
             pltpu.VMEM((3 * C, CELLS + LANES), BF),
             pltpu.VMEM((3 * C, CELLS + 2 * LANES), BF),
@@ -569,7 +619,13 @@
             pltpu.VMEM((3 * C, CELLS + LANES), BF),
             pltpu.VMEM((3 * C, CELLS + 2 * LANES), BF),
             pltpu.VMEM((3 * C, CELLS + 4 * LANES), BF),
+            pltpu.VMEM((C, ROWS, LANES), BF),
+            pltpu.VMEM((C, ROWS, LANES), BF),
+            pltpu.VMEM((3, C), F32),
+            pltpu.VMEM((C,), jnp.int32),
             pltpu.VMEM((3, 9, C, C), BF),
+            pltpu.VMEM((ROWS, C, LANES), BF),
+            pltpu.VMEM((ROWS, C, LANES), BF),
             pltpu.VMEM((C * ROWS, LANES), F32),
             pltpu.VMEM((LANES, 2 * LANES), F32),
             pltpu.VMEM((3, C, CELLS), F32),
@@ -589,18 +645,18 @@
             pltpu.VMEM((3, C, HALF), BF),
             pltpu.VMEM((3, C, HALF), BF),
             pltpu.VMEM((3, 3, BAND, HALF), BF),
-            pltpu.VMEM((3, BAND, HALF), BF),
-            pltpu.VMEM((3, 3, BAND, PART), BF),
-            pltpu.VMEM((3, 4, BAND, PART), BF),
+            pltpu.VMEM((3, 4, BAND, HALF), BF),
+            pltpu.VMEM((3, 4, BAND, HALF), BF),
             pltpu.VMEM((3, C, TOTAL), BF),
-            pltpu.SemaphoreType.DMA((3,)),
+            pltpu.SemaphoreType.DMA((7,)),
+            pltpu.SemaphoreType.DMA((5,)),
             pltpu.SemaphoreType.DMA((6, 6)),
             pltpu.SemaphoreType.DMA((6, 6)),
-            pltpu.SemaphoreType.DMA((3, 20)),
-            pltpu.SemaphoreType.DMA((3, 20)),
+            pltpu.SemaphoreType.DMA((3, 40)),
+            pltpu.SemaphoreType.DMA((3, 40)),
         ],
         compiler_params=pltpu.CompilerParams(
-            collective_id=0, has_side_effects=True, vmem_limit_bytes=48 * 1024 * 1024
+            collective_id=0, has_side_effects=True, vmem_limit_bytes=62 * 1024 * 1024
         ),
         cost_estimate=pl.CostEstimate(
             flops=18 * 9 * C * C * CELLS, bytes_accessed=8 * 1024 * 1024, transcendentals=9 * C * CELLS
@@ -628,7 +684,7 @@
             whole(3, C),
         ),
         scratch_shapes=[pltpu.VMEM((C * ROWS, LANES), F32), pltpu.VMEM((8, C), F32)],
-        compiler_params=pltpu.CompilerParams(vmem_limit_bytes=32 * 1024 * 1024),
+        compiler_params=pltpu.CompilerParams(vmem_limit_bytes=62 * 1024 * 1024),
     )(out, field_grad, summed)
 
 

time: 105 us -> 95.8 us (0.912)
  Pallas kernels: 100 us -> 94.3 us
  local copies, waits for them, and re-layouts: 3.35 us -> 0 us
    pallas_call x1, Pallas kernels: 96.9 us -> 89 us  [shards(): pl.pallas_call(functools.partial(kernel, n), out_shape=(jax.ShapeDtypeStr...]
    unnamed x8 -> x0, local copies, waits for them, and re-layouts: 3.35 us -> none
    pallas_call x1, Pallas kernels: 3.36 us -> 5.27 us  [shards(): pl.pallas_call(finish, grid=(3,), out_shape=(jax.ShapeDtypeStruct((C, ROW...]
where the time goes in v3:
time: 95.8 us; the launch traced here: 95.6 us
  Pallas kernels  94.3 us (98%)
  between operations  1.29 us (1%)
    pallas_call x1, Pallas kernels, shards(): pl.pallas_call(functools.partial(kernel, n), out_shape=(jax.ShapeDtypeStr...  89 us
    pallas_call x1, Pallas kernels, shards(): pl.pallas_call(finish, grid=(3,), out_shape=(jax.ShapeDtypeStruct((C, ROW...  5.27 us

profile of v3, /device:TPU:1, one launch (start us, length us, event | category | flops | bytes accessed | tf_op | source)
XLA Modules:
  0.0 95.6 jit_solution(8417370605614127947)
XLA Ops:
  1.3 89.0 %shard_map.93 = (bf16[8,192,128]{2,1,0:T(8,128)(2,1)}, bf16[8,192,128]{2,1,0:T(8,128)(2,1)}, bf16[3,192,2048]{2,1,0:T(8,128)(2,1)}) custom-call(bf16[192,8,128]{2,1,0:T(8,128)(2,1)} %x_hbm.1, bf16[192,8,128]{2,1,0:T(8,128)(2,1)} %ct_hbm.1, bf16[3,9,192,192]{3,2,1,0:T(8,128)(2,1)} %w_hbm.1, f32[3,192]{1,0:T(4,128)} %bias_hbm.1, s32[1,1]{1,0:T(1,128)S(6)} %copy.10.ocean_ref, ...), custom_call_target="tpu_custom_call" | custom-call | flops 6115295232 | bytes 8388608 | tf_op jit(solution)/shard_map/pallas_call | solution.py:599
  90.3 5.3 %shard_map.94 = (bf16[192,8,128]{2,1,0:T(8,128)(2,1)}, bf16[192,8,128]{2,1,0:T(8,128)(2,1)}, f32[3,9,192,192]{3,2,1,0:T(8,128)}, f32[3,192]{1,0:T(4,128)}) custom-call(bf16[8,192,128]{2,1,0:T(8,128)(2,1)} %get-tuple-element.7.rows_a, bf16[8,192,128]{2,1,0:T(8,128)(2,1)} %get-tuple-element.8.rows_b, bf16[3,192,2048]{2,1,0:T(8,128)(2,1)} %get-tuple-element.9.summed), custom_call_target="tpu_custom_call" | custom-call | tf_op jit(solution)/shard_map/pallas_call | solution.py:666

commit v4 on v3

--- a/solution.py
+++ b/solution.py
@@ -15,6 +15,7 @@
 TOTAL = 2048
 HALF = TOTAL // 2
 BAND = C // 4
+BLOCK = 32
 BF = jnp.bfloat16
 F32 = jnp.float32
 MESH = pl.DeviceIdType.MESH
@@ -97,6 +98,7 @@
     v_side,
     v_over,
     packed,
+    side_tile,
     corner,
     turned,
     rims,
@@ -193,6 +195,7 @@
         def __init__(self, e, buf, d, signed):
             self.e, self.buf, self.d, self.signed = e, buf, d, signed
             self.folds = []
+            self.groups = 4 if d <= 2 else 2
 
         def turn(self, first, last):
             for k in range(first, last):
@@ -214,32 +217,50 @@
             self.folds.append((fold, first, last))
             sends.append((None, fold))
 
-        def pack(self, rows, count):
+        def pack(self, tile, rows, first, last):
             d = self.d
-            tile = jnp.zeros((C, LANES), F32)
-            for r in range(count):
+            for r in range(first, last):
                 at = 2 * d * r
                 here = jnp.logical_and(lane >= at, lane < at + 2 * d)
                 tile = jnp.where(here, pltpu.roll(rows(r).astype(F32), (at + d) % LANES, 1), tile)
             return tile
 
-        def pack_sides(self):
-            tile = self.pack(lambda r: self.buf[0:C, columns(r)], ROWS)
-            packed[self.e] = tile.astype(BF)
+        def dense(self, tile, groups):
+            size = C // groups
+            total = tile[0:size]
+            for q in range(1, groups):
+                piece = tile[q * size : (q + 1) * size]
+                total = total + pltpu.roll(piece, q * LANES // groups, 1)
+            return total.astype(BF)
+
+        def loose(self, total, groups):
+            total = total.astype(F32)
+            return jnp.concatenate(
+                [total]
+                + [pltpu.roll(total, LANES - q * LANES // groups, 1) for q in range(1, groups)],
+                axis=0,
+            )
+
+        def pack_sides(self, first, last):
+            tile = jnp.zeros((C, LANES), F32) if first == 0 else side_tile[...]
+            side_tile[...] = self.pack(
+                tile, lambda r: self.buf[0:C, columns(r)], first, last
+            )
+            if last == ROWS:
+                packed[self.e, 0 : C // self.groups] = self.dense(side_tile[...], self.groups)
 
         def pack_corners(self):
-            tile = self.pack(lambda k: turned[self.e, :, columns(k)], self.d)
-            dense = tile[0:BAND]
-            for q in range(1, 4):
-                dense = dense + pltpu.roll(tile[q * BAND : (q + 1) * BAND], 32 * q, 1)
-            corner[self.e] = dense.astype(BF)
+            tile = self.pack(
+                jnp.zeros((C, LANES), F32), lambda k: turned[self.e, :, columns(k)], 0, self.d
+            )
+            corner[self.e] = self.dense(tile, 4)
 
         def send_sides(self):
             self.sides = []
             for slot, target in enumerate((east, west)):
                 copy = copy_to(
-                    packed.at[self.e],
-                    rims.at[self.e, slot],
+                    packed.at[self.e, pl.ds(0, C // self.groups)],
+                    rims.at[self.e, slot, pl.ds(0, C // self.groups)],
                     ex_send.at[self.e, slot],
                     ex_recv.at[self.e, slot],
                     target,
@@ -271,15 +292,34 @@
             buf[C : 2 * C, columns(row)] = left.astype(BF)
             buf[2 * C : 3 * C, columns(row)] = right.astype(BF)
 
+        def roll_sides(self):
+            buf, d = self.buf, self.d
+            for r in range(ROWS):
+                center = buf[0:C, columns(r)].astype(F32)
+                buf[C : 2 * C, columns(r)] = pltpu.roll(center, d, 1).astype(BF)
+                buf[2 * C : 3 * C, columns(r)] = pltpu.roll(center, LANES - d, 1).astype(BF)
+
         def receive_sides(self):
+            buf, d = self.buf, self.d
             for copy in self.sides:
                 copy.wait_recv()
-            low = lax.rem(lane, 2 * self.d) < self.d
+            size = C // self.groups
+            low = lax.rem(lane, 2 * d) < d
             rim = jnp.where(
-                low, rims[self.e, 0].astype(F32), rims[self.e, 1].astype(F32)
-            )
-            for r in range(ROWS):
-                self.unpack(rim, r, r)
+                low,
+                self.loose(rims[self.e, 0, 0:size], self.groups),
+                self.loose(rims[self.e, 1, 0:size], self.groups),
+            )
+            for r in range(ROWS + 1):
+                edge = pltpu.roll(rim, (-2 * d * r) % LANES, 1) if r > 0 else rim
+                if r < ROWS:
+                    old = buf[C : 2 * C, columns(r)].astype(F32)
+                    buf[C : 2 * C, columns(r)] = jnp.where(lane < d, edge, old).astype(BF)
+                if r > 0:
+                    old = buf[2 * C : 3 * C, columns(r - 1)].astype(F32)
+                    buf[2 * C : 3 * C, columns(r - 1)] = jnp.where(
+                        lane >= LANES - d, edge, old
+                    ).astype(BF)
 
         def receive_corners(self):
             for slot, (away, copy) in enumerate(self.turns):
@@ -293,15 +333,7 @@
                     corners[self.e, slot] = corner[self.e]
 
             low = lax.rem(lane, 2 * self.d) < self.d
-            tiles = []
-            for slot in range(2):
-                dense = corners[self.e, slot].astype(F32)
-                tiles.append(
-                    jnp.concatenate(
-                        [dense] + [pltpu.roll(dense, LANES - 32 * q, 1) for q in range(1, 4)],
-                        axis=0,
-                    )
-                )
+            tiles = [self.loose(corners[self.e, slot], 4) for slot in range(2)]
             self.rim = jnp.where(low, tiles[0], tiles[1])
 
         def receive_fold(self, number):
@@ -394,6 +426,23 @@
         store(full.at[l], dw_hbm.at[l])
         yield
 
+    def weight_sums(l, delta, stored):
+        d = 2**l
+        rest = CELLS - d * LANES
+        for a in range(3):
+            partial[l, :, a * WIDE + 512 : (a + 1) * WIDE] = jnp.zeros((C, LANES), F32)
+        partial[l, :, 0:576] = dot_nt(delta[0:C, d * LANES : CELLS], stored[:, 0:rest])
+        partial[l, :, 640:1216] = dot_nt(delta[0:C, 0:CELLS], stored[:, 0:CELLS])
+        partial[l, :, 1280:1856] = dot_nt(
+            delta[0:C, 0:CELLS], stored[:, d * LANES : CELLS + d * LANES]
+        )
+        partial[l, :, 1920:2048] = jnp.broadcast_to(
+            jnp.sum(delta[0:C, 0:CELLS].astype(F32), axis=1, keepdims=True), (C, LANES)
+        )
+        reduction = all_reduce(l)
+        next(reduction)
+        return reduction
+
     def prepare_forward(l):
         for a in range(3):
             w_side[l, a, :, 0:C] = w_ref[l, 3 * a]
@@ -419,7 +468,7 @@
         s0[0:C, columns(r)] = (row * mask).astype(BF)
     rim = Rims(0, s0, 1, True)
     rim.turn(0, 1)
-    rim.pack_sides()
+    rim.pack_sides(0, ROWS)
     rim.pack_corners()
     loads[0].wait()
     prepare_forward(0)
@@ -445,6 +494,7 @@
         acc[:, d * LANES : CELLS] += dot(w_ref[l, 1], buf[0:C, 0:rest])
         if l < 2:
             prepare_forward(l + 1)
+        rim.roll_sides()
         prepare_backward(2 - l)
         rim.receive_sides()
         acc[...] += dot(w_side[l, 1], buf[C : 3 * C, 0:CELLS])
@@ -471,6 +521,7 @@
             later.send_fold(d, 2 * d)
         else:
             later = Rims(3, t2, d, False)
+        later.pack_sides(0, ROWS - d)
         rim.receive_corners()
         for number in range(len(rim.folds)):
             rim.receive_fold(number)
@@ -487,36 +538,34 @@
         else:
             rim.send_fold(d // 2, d)
             rim.send_fold(0, d // 2)
-        rim.pack_sides()
+        rim.pack_sides(ROWS - d, ROWS)
         rim.send_sides()
 
     store(out_ref, out_hbm)
-    running = []
+    reductions = {}
     for l in (2, 1, 0):
         d = 2**l
         rest = CELLS - d * LANES
         stored = forward_buffers[l]
         buf = backward_buffers[l]
-        for reduction in running:
-            next(reduction)
-        partial[l, :, 512:640] = jnp.zeros((C, LANES), F32)
-        partial[l, :, 1152:1280] = jnp.zeros((C, LANES), F32)
-        partial[l, :, 1792:1920] = jnp.zeros((C, LANES), F32)
-        partial[l, :, 0:576] = dot_nt(buf[0:C, d * LANES : CELLS], stored[:, 0:rest])
-        partial[l, :, 640:1216] = dot_nt(buf[0:C, 0:CELLS], stored[:, 0:CELLS])
-        partial[l, :, 1280:1856] = dot_nt(
-            buf[0:C, 0:CELLS], stored[:, d * LANES : CELLS + d * LANES]
-        )
-        partial[l, :, 1920:2048] = jnp.broadcast_to(
-            jnp.sum(buf[0:C, 0:CELLS].astype(F32), axis=1, keepdims=True), (C, LANES)
-        )
-        reduction = all_reduce(l)
-        next(reduction)
-        running.append(reduction)
+        if l == 0:
+            reductions[0] = weight_sums(0, buf, stored)
+            rim.pack_sides(0, ROWS)
+            rim.send_sides()
+            for older in (0, 1, 2):
+                next(reductions[older])
+        else:
+            reductions[l] = weight_sums(l, buf, stored)
+            for older in range(l + 1, 3):
+                next(reductions[older])
         acc[...] = dot(v_mid[l, 1], buf[0:C, 0:CELLS])
         acc[:, d * LANES : CELLS] += dot(v_mid[l, 2], buf[0:C, 0:rest])
         acc[:, 0:rest] += dot(v_mid[l, 0], buf[0:C, d * LANES : CELLS])
+        rim.roll_sides()
         rim.receive_sides()
+        if l == 0:
+            for older in (0, 1, 2):
+                next(reductions[older])
         acc[...] += dot(v_side[l, 1], buf[C : 3 * C, 0:CELLS])
         acc[:, d * LANES : CELLS] += dot(v_side[l, 2], buf[C : 3 * C, 0:rest])
         acc[:, 0:rest] += dot(v_side[l, 0], buf[C : 3 * C, d * LANES : CELLS])
@@ -533,8 +582,9 @@
                     fg_ref[r] = g[:, r * LANES - first : (r + 1) * LANES - first].astype(BF)
 
         descend(0, rest)
-        for reduction in running:
-            next(reduction)
+        if l > 0:
+            for older in range(l, 3):
+                next(reductions[older])
         rim.receive_corners()
         middle = d // 2
         for number, (fold, first, last) in enumerate(rim.folds):
@@ -556,11 +606,13 @@
                     later.send_fold(0, 1)
         if l > 0:
             rim = later
-            rim.pack_sides()
+        if l > 1:
+            rim.pack_sides(0, ROWS)
             rim.send_sides()
 
     store(fg_ref, fg_hbm)
     done = object()
+    running = [reductions[l] for l in range(3)]
     while running:
         running = [reduction for reduction in running if next(reduction, done) is not done]
     for condition, copy in sends:
@@ -576,21 +628,23 @@
         copy.wait()
 
 
-def finish(rows_a, rows_b, summed, out_a, out_b, kernel_grad, bias_grad, spread_rows, bias_rows):
-    l = pl.program_id(0)
-    for a in range(3):
-        for b in range(3):
-            first = a * WIDE + (1, 0, 2)[b] * C
-            kernel_grad[0, 3 * a + b] = summed[0, :, first : first + C].astype(F32)
-    bias_rows[pl.ds(l, 1), :] = summed[0, :, 3 * WIDE : TOTAL].astype(F32).T[0:1]
-    bias_grad[...] = bias_rows[0:3]
-    for step, rows, out in ((0, rows_a, out_a), (1, rows_b, out_b)):
-
-        @pl.when(l == step)
-        def _():
-            for r in range(ROWS):
-                spread_rows[pl.ds(r, C, stride=ROWS), :] = rows[r].astype(F32)
-            out[...] = spread_rows[...].reshape(C, ROWS, LANES).astype(BF)
+def finish(
+    rows_a, rows_b, summed, last, out_a, out_b, kernel_grad, bias_grad, spread_rows
+):
+    for l in range(3):
+        for a in range(3):
+            for b in range(3):
+                first = a * WIDE + (1, 0, 2)[b] * C
+                kernel_grad[l, 3 * a + b] = summed[l, :, first : first + C].astype(F32)
+    for rows, out in ((rows_a, out_a), (rows_b, out_b)):
+        for r in range(ROWS):
+            spread_rows[pl.ds(r, BLOCK, stride=ROWS), :] = rows[r].astype(F32)
+        out[...] = spread_rows[...].reshape(BLOCK, ROWS, LANES).astype(BF)
+
+    @pl.when(pl.program_id(0) == 0)
+    def _():
+        for l in range(3):
+            bias_grad[l : l + 1, :] = last[l].astype(F32).T[0:1]
 
 
 def shards(fields, cotangent, weights, biases, ocean_tiles, velocity_mask):
@@ -636,6 +690,7 @@
             pltpu.VMEM((3, 3, C, 2 * C), BF),
             pltpu.VMEM((3, C, 3 * C), BF),
             pltpu.VMEM((6, C, LANES), BF),
+            pltpu.VMEM((C, LANES), F32),
             pltpu.VMEM((6, BAND, LANES), BF),
             pltpu.VMEM((6, C, 4 * LANES), BF),
             pltpu.VMEM((6, 2, C, LANES), BF),
@@ -662,10 +717,9 @@
             flops=18 * 9 * C * C * CELLS, bytes_accessed=8 * 1024 * 1024, transcendentals=9 * C * CELLS
         ),
     )(fields, cotangent, weights, biases, ocean_tiles, velocity_mask)
-    whole = lambda *shape: pl.BlockSpec(shape, lambda l: (0,) * len(shape))
     return pl.pallas_call(
         finish,
-        grid=(3,),
+        grid=(C // BLOCK,),
         out_shape=(
             jax.ShapeDtypeStruct((C, ROWS, LANES), BF),
             jax.ShapeDtypeStruct((C, ROWS, LANES), BF),
@@ -673,19 +727,20 @@
             jax.ShapeDtypeStruct((3, C), F32),
         ),
         in_specs=[
-            whole(ROWS, C, LANES),
-            whole(ROWS, C, LANES),
-            pl.BlockSpec((1, C, TOTAL), lambda l: (l, 0, 0)),
+            pl.BlockSpec((ROWS, BLOCK, LANES), lambda i: (0, i, 0)),
+            pl.BlockSpec((ROWS, BLOCK, LANES), lambda i: (0, i, 0)),
+            pl.BlockSpec((3, BLOCK, TOTAL), lambda i: (0, i, 0)),
+            pl.BlockSpec((3, C, LANES), lambda i: (0, 0, TOTAL // LANES - 1)),
         ],
         out_specs=(
-            whole(C, ROWS, LANES),
-            whole(C, ROWS, LANES),
-            pl.BlockSpec((1, 9, C, C), lambda l: (l, 0, 0, 0)),
-            whole(3, C),
+            pl.BlockSpec((BLOCK, ROWS, LANES), lambda i: (i, 0, 0)),
+            pl.BlockSpec((BLOCK, ROWS, LANES), lambda i: (i, 0, 0)),
+            pl.BlockSpec((3, 9, BLOCK, C), lambda i: (0, 0, i, 0)),
+            pl.BlockSpec((3, C), lambda i: (0, 0)),
         ),
-        scratch_shapes=[pltpu.VMEM((C * ROWS, LANES), F32), pltpu.VMEM((8, C), F32)],
+        scratch_shapes=[pltpu.VMEM((BLOCK * ROWS, LANES), F32)],
         compiler_params=pltpu.CompilerParams(vmem_limit_bytes=62 * 1024 * 1024),
-    )(out, field_grad, summed)
+    )(out, field_grad, summed, summed)
 
 
 def solution(mesh):

time: 95.8 us -> 87.7 us (0.915)
  Pallas kernels: 94.3 us -> 86.1 us
    pallas_call x1, Pallas kernels: 89 us -> 79.8 us  [shards(): pl.pallas_call(functools.partial(kernel, n), out_shape=(jax.ShapeDtypeStr...]
    pallas_call x1, Pallas kernels: 5.27 us -> 6.25 us  [shards(): pl.pallas_call(finish, grid=(C // BLOCK,), out_shape=(jax.ShapeDtypeStruc...]
where the time goes in v4:
time: 87.7 us; the launch traced here: 87.5 us
  Pallas kernels  86.1 us (98%)
  between operations  1.42 us (2%)
    pallas_call x1, Pallas kernels, shards(): pl.pallas_call(functools.partial(kernel, n), out_shape=(jax.ShapeDtypeStr...  79.8 us
    pallas_call x1, Pallas kernels, shards(): pl.pallas_call(finish, grid=(C // BLOCK,), out_shape=(jax.ShapeDtypeStruc...  6.25 us

profile of v4, /device:TPU:1, one launch (start us, length us, event | category | flops | bytes accessed | tf_op | source)
XLA Modules:
  0.0 87.5 jit_solution(6263079413658184505)
XLA Ops:
  1.3 79.8 %shard_map.93 = (bf16[8,192,128]{2,1,0:T(8,128)(2,1)}, bf16[8,192,128]{2,1,0:T(8,128)(2,1)}, bf16[3,192,2048]{2,1,0:T(8,128)(2,1)}) custom-call(bf16[192,8,128]{2,1,0:T(8,128)(2,1)} %x_hbm.1, bf16[192,8,128]{2,1,0:T(8,128)(2,1)} %ct_hbm.1, bf16[3,9,192,192]{3,2,1,0:T(8,128)(2,1)} %w_hbm.1, f32[3,192]{1,0:T(4,128)} %bias_hbm.1, s32[1,1]{1,0:T(1,128)S(6)} %copy.10.ocean_ref, ...), custom_call_target="tpu_custom_call" | custom-call | flops 6115295232 | bytes 8388608 | tf_op jit(solution)/shard_map/pallas_call | solution.py:653
  81.1 6.3 %shard_map.94 = (bf16[192,8,128]{2,1,0:T(8,128)(2,1)}, bf16[192,8,128]{2,1,0:T(8,128)(2,1)}, f32[3,9,192,192]{3,2,1,0:T(8,128)}, f32[3,192]{1,0:T(4,128)}) custom-call(bf16[8,192,128]{2,1,0:T(8,128)(2,1)} %get-tuple-element.7.rows_a, bf16[8,192,128]{2,1,0:T(8,128)(2,1)} %get-tuple-element.8.rows_b, bf16[3,192,2048]{2,1,0:T(8,128)(2,1)} %get-tuple-element.9.summed.last, ...), custom_call_target="tpu_custom_call" | custom-call | tf_op jit(solution)/shard_map/pallas_call | solution.py:720

commit v5 on v4

--- a/solution.py
+++ b/solution.py
@@ -15,7 +15,6 @@
 TOTAL = 2048
 HALF = TOTAL // 2
 BAND = C // 4
-BLOCK = 32
 BF = jnp.bfloat16
 F32 = jnp.float32
 MESH = pl.DeviceIdType.MESH
@@ -629,22 +628,52 @@
 
 
 def finish(
-    rows_a, rows_b, summed, last, out_a, out_b, kernel_grad, bias_grad, spread_rows
+    rows_a,
+    rows_b,
+    summed,
+    out_a,
+    out_b,
+    kernel_grad,
+    bias_grad,
+    rows,
+    sums,
+    spread_rows,
+    cells,
+    kernels,
+    bias_rows,
+    in_sem,
+    out_sem,
 ):
+    loads = [pltpu.make_async_copy(summed.at[l], sums.at[l], in_sem.at[l]) for l in range(3)]
+    for number, src in enumerate((rows_a, rows_b)):
+        loads.append(pltpu.make_async_copy(src, rows.at[number], in_sem.at[3 + number]))
+    for load in loads:
+        load.start()
+    stores = []
+
+    def store(src, dst):
+        copy = pltpu.make_async_copy(src, dst, out_sem.at[len(stores)])
+        copy.start()
+        stores.append(copy)
+
     for l in range(3):
+        loads[l].wait()
         for a in range(3):
             for b in range(3):
                 first = a * WIDE + (1, 0, 2)[b] * C
-                kernel_grad[l, 3 * a + b] = summed[l, :, first : first + C].astype(F32)
-    for rows, out in ((rows_a, out_a), (rows_b, out_b)):
+                kernels[l, 3 * a + b] = sums[l, :, first : first + C].astype(F32)
+            taps = pl.ds(3 * a, 3)
+            store(kernels.at[l, taps], kernel_grad.at[l, taps])
+        bias_rows[l : l + 1, :] = sums[l, :, 3 * WIDE : TOTAL].astype(F32).T[0:1]
+    store(bias_rows, bias_grad)
+    for number, dst in enumerate((out_a, out_b)):
+        loads[3 + number].wait()
         for r in range(ROWS):
-            spread_rows[pl.ds(r, BLOCK, stride=ROWS), :] = rows[r].astype(F32)
-        out[...] = spread_rows[...].reshape(BLOCK, ROWS, LANES).astype(BF)
-
-    @pl.when(pl.program_id(0) == 0)
-    def _():
-        for l in range(3):
-            bias_grad[l : l + 1, :] = last[l].astype(F32).T[0:1]
+            spread_rows[pl.ds(r, C, stride=ROWS), :] = rows[number, r].astype(F32)
+        cells[number] = spread_rows[...].reshape(C, ROWS, LANES).astype(BF)
+        store(cells.at[number], dst)
+    for copy in stores:
+        copy.wait()
 
 
 def shards(fields, cotangent, weights, biases, ocean_tiles, velocity_mask):
@@ -719,28 +748,26 @@
     )(fields, cotangent, weights, biases, ocean_tiles, velocity_mask)
     return pl.pallas_call(
         finish,
-        grid=(C // BLOCK,),
         out_shape=(
             jax.ShapeDtypeStruct((C, ROWS, LANES), BF),
             jax.ShapeDtypeStruct((C, ROWS, LANES), BF),
             jax.ShapeDtypeStruct((3, 9, C, C), F32),
             jax.ShapeDtypeStruct((3, C), F32),
         ),
-        in_specs=[
-            pl.BlockSpec((ROWS, BLOCK, LANES), lambda i: (0, i, 0)),
-            pl.BlockSpec((ROWS, BLOCK, LANES), lambda i: (0, i, 0)),
-            pl.BlockSpec((3, BLOCK, TOTAL), lambda i: (0, i, 0)),
-            pl.BlockSpec((3, C, LANES), lambda i: (0, 0, TOTAL // LANES - 1)),
+        in_specs=[hbm] * 3,
+        out_specs=(hbm,) * 4,
+        scratch_shapes=[
+            pltpu.VMEM((2, ROWS, C, LANES), BF),
+            pltpu.VMEM((3, C, TOTAL), BF),
+            pltpu.VMEM((C * ROWS, LANES), F32),
+            pltpu.VMEM((2, C, ROWS, LANES), BF),
+            pltpu.VMEM((3, 9, C, C), F32),
+            pltpu.VMEM((3, C), F32),
+            pltpu.SemaphoreType.DMA((5,)),
+            pltpu.SemaphoreType.DMA((12,)),
         ],
-        out_specs=(
-            pl.BlockSpec((BLOCK, ROWS, LANES), lambda i: (i, 0, 0)),
-            pl.BlockSpec((BLOCK, ROWS, LANES), lambda i: (i, 0, 0)),
-            pl.BlockSpec((3, 9, BLOCK, C), lambda i: (0, 0, i, 0)),
-            pl.BlockSpec((3, C), lambda i: (0, 0)),
-        ),
-        scratch_shapes=[pltpu.VMEM((BLOCK * ROWS, LANES), F32)],
         compiler_params=pltpu.CompilerParams(vmem_limit_bytes=62 * 1024 * 1024),
-    )(out, field_grad, summed, summed)
+    )(out, field_grad, summed)
 
 
 def solution(mesh):

time: 87.7 us -> 85.4 us (0.974)
  Pallas kernels: 86.1 us -> 83.8 us
    pallas_call x1, Pallas kernels: 6.25 us -> 3.98 us  [shards(): pl.pallas_call(finish, out_shape=(jax.ShapeDtypeStruct((C, ROWS, LANES),...]
where the time goes in v5:
time: 85.4 us; the launch traced here: 85.2 us
  Pallas kernels  83.8 us (98%)
  between operations  1.45 us (2%)
    pallas_call x1, Pallas kernels, shards(): pl.pallas_call(functools.partial(kernel, n), out_shape=(jax.ShapeDtypeStr...  79.8 us
    pallas_call x1, Pallas kernels, shards(): pl.pallas_call(finish, out_shape=(jax.ShapeDtypeStruct((C, ROWS, LANES),...  3.98 us

profile of v5, /device:TPU:1, one launch (start us, length us, event | category | flops | bytes accessed | tf_op | source)
XLA Modules:
  0.0 85.2 jit_solution(5989608577405928443)
XLA Ops:
  1.3 79.8 %shard_map.93 = (bf16[8,192,128]{2,1,0:T(8,128)(2,1)}, bf16[8,192,128]{2,1,0:T(8,128)(2,1)}, bf16[3,192,2048]{2,1,0:T(8,128)(2,1)}) custom-call(bf16[192,8,128]{2,1,0:T(8,128)(2,1)} %x_hbm.1, bf16[192,8,128]{2,1,0:T(8,128)(2,1)} %ct_hbm.1, bf16[3,9,192,192]{3,2,1,0:T(8,128)(2,1)} %w_hbm.1, f32[3,192]{1,0:T(4,128)} %bias_hbm.1, s32[1,1]{1,0:T(1,128)S(6)} %copy.10.ocean_ref, ...), custom_call_target="tpu_custom_call" | custom-call | flops 6115295232 | bytes 8388608 | tf_op jit(solution)/shard_map/pallas_call | solution.py:682
  81.1 4.0 %shard_map.94 = (bf16[192,8,128]{2,1,0:T(8,128)(2,1)}, bf16[192,8,128]{2,1,0:T(8,128)(2,1)}, f32[3,9,192,192]{3,2,1,0:T(8,128)}, f32[3,192]{1,0:T(4,128)}) custom-call(bf16[8,192,128]{2,1,0:T(8,128)(2,1)} %get-tuple-element.7.rows_a, bf16[8,192,128]{2,1,0:T(8,128)(2,1)} %get-tuple-element.8.rows_b, bf16[3,192,2048]{2,1,0:T(8,128)(2,1)} %get-tuple-element.9.summed), custom_call_target="tpu_custom_call" | custom-call | tf_op jit(solution)/shard_map/pallas_call | solution.py:749

commit v6 on v5

--- a/solution.py
+++ b/solution.py
@@ -98,6 +98,10 @@
     v_over,
     packed,
     side_tile,
+    own_tile,
+    strip_cols,
+    w_own,
+    w_turn,
     corner,
     turned,
     rims,
@@ -190,6 +194,40 @@
     def columns(row, count=1):
         return slice(row * LANES, (row + count) * LANES)
 
+    def dense(tile, groups):
+        size = C // groups
+        total = tile[0:size]
+        for q in range(1, groups):
+            piece = tile[q * size : (q + 1) * size]
+            total = total + pltpu.roll(piece, q * LANES // groups, 1)
+        return total.astype(BF)
+
+    def loose(total, groups):
+        total = total.astype(F32)
+        return jnp.concatenate(
+            [total]
+            + [pltpu.roll(total, LANES - q * LANES // groups, 1) for q in range(1, groups)],
+            axis=0,
+        )
+
+    def slots(rows, count):
+        tile = jnp.zeros((C, LANES), F32)
+        for r in range(count):
+            here = jnp.logical_and(lane >= 8 * r, lane < 8 * r + 8)
+            tile = jnp.where(here, pltpu.roll(rows(r).astype(F32), (8 * r + 4) % LANES, 1), tile)
+        return tile
+
+    def widen(buf, rim, row, d):
+        center = buf[0:C, columns(row)].astype(F32)
+        left = pltpu.roll(rim, (-(8 * row + 4 - d)) % LANES, 1)
+        right = pltpu.roll(rim, (-(8 * row + 4 + d)) % LANES, 1)
+        buf[C : 2 * C, columns(row)] = jnp.where(
+            lane < d, left, pltpu.roll(center, d, 1)
+        ).astype(BF)
+        buf[2 * C : 3 * C, columns(row)] = jnp.where(
+            lane >= LANES - d, right, pltpu.roll(center, LANES - d, 1)
+        ).astype(BF)
+
     class Rims:
         def __init__(self, e, buf, d, signed):
             self.e, self.buf, self.d, self.signed = e, buf, d, signed
@@ -224,35 +262,19 @@
                 tile = jnp.where(here, pltpu.roll(rows(r).astype(F32), (at + d) % LANES, 1), tile)
             return tile
 
-        def dense(self, tile, groups):
-            size = C // groups
-            total = tile[0:size]
-            for q in range(1, groups):
-                piece = tile[q * size : (q + 1) * size]
-                total = total + pltpu.roll(piece, q * LANES // groups, 1)
-            return total.astype(BF)
-
-        def loose(self, total, groups):
-            total = total.astype(F32)
-            return jnp.concatenate(
-                [total]
-                + [pltpu.roll(total, LANES - q * LANES // groups, 1) for q in range(1, groups)],
-                axis=0,
-            )
-
         def pack_sides(self, first, last):
             tile = jnp.zeros((C, LANES), F32) if first == 0 else side_tile[...]
             side_tile[...] = self.pack(
                 tile, lambda r: self.buf[0:C, columns(r)], first, last
             )
             if last == ROWS:
-                packed[self.e, 0 : C // self.groups] = self.dense(side_tile[...], self.groups)
+                packed[self.e, 0 : C // self.groups] = dense(side_tile[...], self.groups)
 
         def pack_corners(self):
             tile = self.pack(
                 jnp.zeros((C, LANES), F32), lambda k: turned[self.e, :, columns(k)], 0, self.d
             )
-            corner[self.e] = self.dense(tile, 4)
+            corner[self.e] = dense(tile, 4)
 
         def send_sides(self):
             self.sides = []
@@ -306,8 +328,8 @@
             low = lax.rem(lane, 2 * d) < d
             rim = jnp.where(
                 low,
-                self.loose(rims[self.e, 0, 0:size], self.groups),
-                self.loose(rims[self.e, 1, 0:size], self.groups),
+                loose(rims[self.e, 0, 0:size], self.groups),
+                loose(rims[self.e, 1, 0:size], self.groups),
             )
             for r in range(ROWS + 1):
                 edge = pltpu.roll(rim, (-2 * d * r) % LANES, 1) if r > 0 else rim
@@ -332,7 +354,7 @@
                     corners[self.e, slot] = corner[self.e]
 
             low = lax.rem(lane, 2 * self.d) < self.d
-            tiles = [self.loose(corners[self.e, slot], 4) for slot in range(2)]
+            tiles = [loose(corners[self.e, slot], 4) for slot in range(2)]
             self.rim = jnp.where(low, tiles[0], tiles[1])
 
         def receive_fold(self, number):
@@ -466,11 +488,22 @@
         row = spread_rows[pl.ds(r, C, stride=ROWS), :]
         s0[0:C, columns(r)] = (row * mask).astype(BF)
     rim = Rims(0, s0, 1, True)
-    rim.turn(0, 1)
-    rim.pack_sides(0, ROWS)
-    rim.pack_corners()
+    rim.turn(0, 3)
+    own_tile[...] = slots(lambda r: s0[0:C, columns(r)], ROWS)
+    packed[0, 0 : C // 2] = dense(own_tile[...], 2)
+    packed[0, C // 2 : C // 2 + 16] = jnp.full((16, LANES), mask, F32).astype(BF)
+    tile = slots(lambda k: turned[0, :, columns(k)], 3)
+    tile = jnp.where(jnp.logical_and(lane >= 24, lane < 32), mask, tile)
+    corner[0] = dense(tile, 4)
     loads[0].wait()
     prepare_forward(0)
+    for a in range(3):
+        for place, b in enumerate((1, 0, 2)):
+            part = slice(place * C, (place + 1) * C)
+            w_own[a, :, part] = w_ref[0, 3 * a + b]
+            w_turn[a, :, part] = (w_ref[0, 8 - 3 * a - b].astype(F32) * cols_ref[3:4, 0:C]).astype(
+                BF
+            )
     small[3].wait()
     spread_rows[...] = ct_ref[...].astype(F32).reshape(C * ROWS, LANES)
     for r in range(ROWS):
@@ -480,65 +513,188 @@
     pl.semaphore_wait(
         barrier, len(partners) + a_away.astype(jnp.int32) + b_away.astype(jnp.int32)
     )
+    sides = [
+        copy_to(
+            packed.at[0, pl.ds(0, C // 2 + 16)],
+            rims.at[0, slot, pl.ds(0, C // 2 + 16)],
+            ex_send.at[0, slot],
+            ex_recv.at[0, slot],
+            target,
+        )
+        for slot, target in enumerate((east, west))
+    ]
+    over = copy_to(
+        corner.at[0], corners.at[0, 2], ex_send.at[0, 5], ex_recv.at[0, 5], mirror
+    )
+    for copy in sides + [over]:
+        copy.start()
+        sends.append((None, copy))
     rim.send_corners()
-    rim.send_fold(0, 1)
+    rim.send_fold(0, 3)
+
+    def activate(l, buf, first, last):
+        v = acc[:, first:last]
+        s = jax.nn.sigmoid(v)
+        after = mask * (buf[0:C, first:last].astype(F32) + v * s)
+        s = s * (1.0 + v * (1.0 - s))
+        slope[l, :, first:last] = s
+        if l < 2:
+            forward_buffers[l + 1][0:C, first:last] = after.astype(BF)
+        else:
+            for r in range(first // LANES, last // LANES):
+                out_ref[r] = after[:, r * LANES - first : (r + 1) * LANES - first].astype(BF)
+            t2[0:C, first:last] = (grad[:, first:last] * s).astype(BF)
+
+    rest = CELLS - LANES
+    acc[...] = dot(w_ref[0, 4], s0[0:C, 0:CELLS]) + bias_cols[0]
+    acc[:, 0:rest] += dot(w_ref[0, 7], s0[0:C, LANES:CELLS])
+    acc[:, LANES:CELLS] += dot(w_ref[0, 1], s0[0:C, 0:rest])
+    prepare_forward(1)
+    prepare_backward(2)
+    for copy in sides:
+        copy.wait_recv()
+    low = lax.rem(lane, 8) < 4
+    west_tile = loose(rims[0, 0, 0 : C // 2], 2)
+    east_tile = loose(rims[0, 1, 0 : C // 2], 2)
+    rim_tile = jnp.where(low, west_tile, east_tile)
+    for r in range(ROWS):
+        widen(s0, rim_tile, r, 1)
+    acc[...] += dot(w_side[0, 1], s0[C : 3 * C, 0:CELLS])
+    acc[:, 0:rest] += dot(w_side[0, 2], s0[C : 3 * C, LANES:CELLS])
+    acc[:, LANES:CELLS] += dot(w_side[0, 0], s0[C : 3 * C, 0:rest])
+    activate(0, s0, 0, rest)
+
+    for slot, (away, copy) in enumerate(rim.turns):
+
+        @pl.when(away)
+        def _():
+            copy.wait_recv()
+
+        @pl.when(jnp.logical_not(away))
+        def _():
+            corners[0, slot] = corner[0]
+
+    over.wait_recv()
+    far_a, far_b, far = (pltpu.roll(loose(corners[0, slot], 4), 64, 1) for slot in range(3))
+    inside = lane < 64
+    beyond = lane < 88
+    strips = [
+        jnp.where(
+            inside,
+            jnp.where(low, west_tile, own_tile[...]),
+            jnp.where(beyond, jnp.where(low, far_a, far), 0.0),
+        ),
+        jnp.where(
+            inside,
+            jnp.where(low, own_tile[...], east_tile),
+            jnp.where(beyond, jnp.where(low, far, far_b), 0.0),
+        ),
+    ]
+    rim_tile = jnp.where(low, strips[0], strips[1])
+    for a in range(3):
+        for place, b in enumerate((0, -1, 1)):
+            shift = (-(8 * (a - 1) + b)) % LANES
+            for side in range(2):
+                moved = pltpu.roll(strips[side], shift, 1) if shift else strips[side]
+                strip_cols[
+                    (3 * a + place) * C : (3 * a + place + 1) * C, columns(side)
+                ] = moved.astype(BF)
+    own_sum = bias_cols[0]
+    far_sum = bias_cols[0]
+    for a in range(3):
+        taps = strip_cols[3 * C * a : 3 * C * (a + 1), :]
+        own_sum = own_sum + dot(w_own[a], taps)
+        far_sum = far_sum + dot(w_turn[a], taps)
+    after = []
+    for side in range(2):
+        v = jnp.where(inside, own_sum[:, columns(side)], far_sum[:, columns(side)])
+        v = v * jax.nn.sigmoid(v)
+        v = jnp.where(inside, v, v * flip_sign)
+        near_mask = rims[0, side, C // 2 : C // 2 + 1, 0:1].astype(F32)
+        far_mask = corners[0, side, 0:1, 24:25].astype(F32)
+        side_mask = jnp.where(inside[0:1], near_mask, far_mask)
+        after.append((side_mask * (strips[side] + v)).astype(BF).astype(F32))
+    next_tile = jnp.where(low, after[0], after[1])
+    for r in range(ROWS - 1):
+        widen(s1, next_tile, r, 2)
+
+    def second(first, last):
+        step = 2 * LANES
+        acc[:, first:last] = (
+            dot(w_ref[1, 4], s1[0:C, first:last])
+            + dot(w_side[1, 1], s1[C : 3 * C, first:last])
+            + bias_cols[1]
+        )
+        acc[:, first:last] += dot(w_ref[1, 7], s1[0:C, first + step : last + step]) + dot(
+            w_side[1, 2], s1[C : 3 * C, first + step : last + step]
+        )
+        low_row = max(first, step)
+        acc[:, low_row:last] += dot(w_ref[1, 1], s1[0:C, low_row - step : last - step]) + dot(
+            w_side[1, 0], s1[C : 3 * C, low_row - step : last - step]
+        )
+        activate(1, s1, first, last)
+
+    second(0, 4 * LANES)
+    later = Rims(2, s2, 4, True)
+    later.pack_sides(0, 4)
+    prepare_forward(2)
+
+    rim.folds[0][0].wait_recv()
+    for k in range(3):
+        widen(s0, rim_tile, ROWS + k, 1)
+    acc[:, rest:CELLS] += dot(w_ref[0, 7], s0[0:C, CELLS : CELLS + LANES]) + dot(
+        w_side[0, 2], s0[C : 3 * C, CELLS : CELLS + LANES]
+    )
+    activate(0, s0, rest, CELLS)
+    v = bias_cols[0]
+    for a in range(3):
+        v = v + dot(w_turn[a], s0[:, columns(7 + a, 2)])
+    v = v * jax.nn.sigmoid(v) * flip_sign
+    far_mask = corners[0, 2, 0:1, 24:25].astype(F32)
+    s1[0:C, columns(ROWS, 2)] = (far_mask * (s0[0:C, columns(ROWS, 2)].astype(F32) + v)).astype(BF)
+    for r in range(ROWS - 1, ROWS + 2):
+        widen(s1, next_tile, r, 2)
+    second(4 * LANES, CELLS)
+    rim = later
+    rim.turn(0, 4)
+    rim.pack_corners()
+    rim.send_corners()
+    rim.send_fold(0, 2)
+    rim.send_fold(2, 4)
+    rim.pack_sides(4, ROWS)
     rim.send_sides()
 
-    for l in range(3):
-        d = 2**l
-        rest = CELLS - d * LANES
-        buf = forward_buffers[l]
-        acc[...] = dot(w_ref[l, 4], buf[0:C, 0:CELLS]) + bias_cols[l]
-        acc[:, 0:rest] += dot(w_ref[l, 7], buf[0:C, d * LANES : CELLS])
-        acc[:, d * LANES : CELLS] += dot(w_ref[l, 1], buf[0:C, 0:rest])
-        if l < 2:
-            prepare_forward(l + 1)
-        rim.roll_sides()
-        prepare_backward(2 - l)
-        rim.receive_sides()
-        acc[...] += dot(w_side[l, 1], buf[C : 3 * C, 0:CELLS])
-        acc[:, 0:rest] += dot(w_side[l, 2], buf[C : 3 * C, d * LANES : CELLS])
-        acc[:, d * LANES : CELLS] += dot(w_side[l, 0], buf[C : 3 * C, 0:rest])
-
-        def activate(first, last):
-            v = acc[:, first:last]
-            s = jax.nn.sigmoid(v)
-            after = mask * (buf[0:C, first:last].astype(F32) + v * s)
-            s = s * (1.0 + v * (1.0 - s))
-            slope[l, :, first:last] = s
-            if l < 2:
-                forward_buffers[l + 1][0:C, first:last] = after.astype(BF)
-            else:
-                for r in range(first // LANES, last // LANES):
-                    out_ref[r] = after[:, r * LANES - first : (r + 1) * LANES - first].astype(BF)
-                t2[0:C, first:last] = (grad[:, first:last] * s).astype(BF)
-
-        activate(0, rest)
-        if l < 2:
-            later = Rims(l + 1, forward_buffers[l + 1], 2 * d, True)
-            later.turn(d, 2 * d)
-            later.send_fold(d, 2 * d)
-        else:
-            later = Rims(3, t2, d, False)
-        later.pack_sides(0, ROWS - d)
-        rim.receive_corners()
-        for number in range(len(rim.folds)):
-            rim.receive_fold(number)
-        acc[:, rest:CELLS] += dot(w_ref[l, 7], buf[0:C, CELLS : CELLS + d * LANES]) + dot(
-            w_side[l, 2], buf[C : 3 * C, CELLS : CELLS + d * LANES]
-        )
-        activate(rest, CELLS)
-        rim = later
-        rim.turn(0, d)
-        rim.pack_corners()
-        rim.send_corners()
-        if l < 2:
-            rim.send_fold(0, d)
-        else:
-            rim.send_fold(d // 2, d)
-            rim.send_fold(0, d // 2)
-        rim.pack_sides(ROWS - d, ROWS)
-        rim.send_sides()
+    d = 4
+    rest = CELLS - d * LANES
+    acc[...] = dot(w_ref[2, 4], s2[0:C, 0:CELLS]) + bias_cols[2]
+    acc[:, 0:rest] += dot(w_ref[2, 7], s2[0:C, d * LANES : CELLS])
+    acc[:, d * LANES : CELLS] += dot(w_ref[2, 1], s2[0:C, 0:rest])
+    rim.roll_sides()
+    prepare_backward(1)
+    prepare_backward(0)
+    rim.receive_sides()
+    acc[...] += dot(w_side[2, 1], s2[C : 3 * C, 0:CELLS])
+    acc[:, 0:rest] += dot(w_side[2, 2], s2[C : 3 * C, d * LANES : CELLS])
+    acc[:, d * LANES : CELLS] += dot(w_side[2, 0], s2[C : 3 * C, 0:rest])
+    activate(2, s2, 0, rest)
+    later = Rims(3, t2, d, False)
+    later.pack_sides(0, ROWS - d)
+    rim.receive_corners()
+    for number, (fold, first, last) in enumerate(rim.folds):
+        rim.receive_fold(number)
+        top = slice(rest + first * LANES, rest + last * LANES)
+        over = slice(CELLS + first * LANES, CELLS + last * LANES)
+        acc[:, top] += dot(w_ref[2, 7], s2[0:C, over]) + dot(w_side[2, 2], s2[C : 3 * C, over])
+        activate(2, s2, top.start, top.stop)
+        later.turn(d - last, d - first)
+        if number == 0:
+            later.send_fold(d - last, d - first)
+    rim = later
+    rim.pack_corners()
+    rim.send_corners()
+    rim.send_fold(0, d // 2)
+    rim.pack_sides(ROWS - d, ROWS)
+    rim.send_sides()
 
     store(out_ref, out_hbm)
     reductions = {}
@@ -582,8 +738,7 @@
 
         descend(0, rest)
         if l > 0:
-            for older in range(l, 3):
-                next(reductions[older])
+            next(reductions[l])
         rim.receive_corners()
         middle = d // 2
         for number, (fold, first, last) in enumerate(rim.folds):
@@ -696,7 +851,7 @@
         ],
         out_specs=(hbm,) * 3,
         scratch_shapes=[
-            pltpu.VMEM((3 * C, CELLS + LANES), BF),
+            pltpu.VMEM((3 * C, CELLS + 3 * LANES), BF),
             pltpu.VMEM((3 * C, CELLS + 2 * LANES), BF),
             pltpu.VMEM((3 * C, CELLS + 4 * LANES), BF),
             pltpu.VMEM((3 * C, CELLS + LANES), BF),
@@ -720,10 +875,14 @@
             pltpu.VMEM((3, C, 3 * C), BF),
             pltpu.VMEM((6, C, LANES), BF),
             pltpu.VMEM((C, LANES), F32),
+            pltpu.VMEM((C, LANES), F32),
+            pltpu.VMEM((9 * C, 2 * LANES), BF),
+            pltpu.VMEM((3, C, 3 * C), BF),
+            pltpu.VMEM((3, C, 3 * C), BF),
             pltpu.VMEM((6, BAND, LANES), BF),
             pltpu.VMEM((6, C, 4 * LANES), BF),
             pltpu.VMEM((6, 2, C, LANES), BF),
-            pltpu.VMEM((6, 2, BAND, LANES), BF),
+            pltpu.VMEM((6, 3, BAND, LANES), BF),
             pltpu.VMEM((3, C, TOTAL), F32),
             pltpu.VMEM((3, C, HALF), BF),
             pltpu.VMEM((3, C, HALF), BF),

time: 85.4 us -> 82.5 us (0.966)
  Pallas kernels: 83.8 us -> 81 us
    pallas_call x1, Pallas kernels: 79.8 us -> 77 us  [shards(): pl.pallas_call(functools.partial(kernel, n), out_shape=(jax.ShapeDtypeStr...]
where the time goes in v6:
time: 82.5 us; the launch traced here: 82.4 us
  Pallas kernels  81 us (98%)
  between operations  1.45 us (2%)
    pallas_call x1, Pallas kernels, shards(): pl.pallas_call(functools.partial(kernel, n), out_shape=(jax.ShapeDtypeStr...  77 us
    pallas_call x1, Pallas kernels, shards(): pl.pallas_call(finish, out_shape=(jax.ShapeDtypeStruct((C, ROWS, LANES),...  3.98 us

profile of v6, /device:TPU:1, one launch (start us, length us, event | category | flops | bytes accessed | tf_op | source)
XLA Modules:
  0.0 82.4 jit_solution(12182871197991329011)
XLA Ops:
  1.3 77.0 %shard_map.93 = (bf16[8,192,128]{2,1,0:T(8,128)(2,1)}, bf16[8,192,128]{2,1,0:T(8,128)(2,1)}, bf16[3,192,2048]{2,1,0:T(8,128)(2,1)}) custom-call(bf16[192,8,128]{2,1,0:T(8,128)(2,1)} %x_hbm.1, bf16[192,8,128]{2,1,0:T(8,128)(2,1)} %ct_hbm.1, bf16[3,9,192,192]{3,2,1,0:T(8,128)(2,1)} %w_hbm.1, f32[3,192]{1,0:T(4,128)} %bias_hbm.1, s32[1,1]{1,0:T(1,128)S(6)} %copy.10.ocean_ref, ...), custom_call_target="tpu_custom_call" | custom-call | flops 6115295232 | bytes 8388608 | tf_op jit(solution)/shard_map/pallas_call | solution.py:837
  78.3 4.0 %shard_map.94 = (bf16[192,8,128]{2,1,0:T(8,128)(2,1)}, bf16[192,8,128]{2,1,0:T(8,128)(2,1)}, f32[3,9,192,192]{3,2,1,0:T(8,128)}, f32[3,192]{1,0:T(4,128)}) custom-call(bf16[8,192,128]{2,1,0:T(8,128)(2,1)} %get-tuple-element.7.rows_a, bf16[8,192,128]{2,1,0:T(8,128)(2,1)} %get-tuple-element.8.rows_b, bf16[3,192,2048]{2,1,0:T(8,128)(2,1)} %get-tuple-element.9.summed), custom_call_target="tpu_custom_call" | custom-call | tf_op jit(solution)/shard_map/pallas_call | solution.py:908

commit v7 on v6

--- a/solution.py
+++ b/solution.py
@@ -317,8 +317,10 @@
             buf, d = self.buf, self.d
             for r in range(ROWS):
                 center = buf[0:C, columns(r)].astype(F32)
-                buf[C : 2 * C, columns(r)] = pltpu.roll(center, d, 1).astype(BF)
-                buf[2 * C : 3 * C, columns(r)] = pltpu.roll(center, LANES - d, 1).astype(BF)
+                left = jnp.where(lane < d, 0.0, pltpu.roll(center, d, 1))
+                right = jnp.where(lane >= LANES - d, 0.0, pltpu.roll(center, LANES - d, 1))
+                buf[C : 2 * C, columns(r)] = left.astype(BF)
+                buf[2 * C : 3 * C, columns(r)] = right.astype(BF)
 
         def receive_sides(self):
             buf, d = self.buf, self.d
@@ -342,6 +344,32 @@
                         lane >= LANES - d, edge, old
                     ).astype(BF)
 
+        def receive_edges(self, l):
+            d = self.d
+            for copy in self.sides:
+                copy.wait_recv()
+            size = C // self.groups
+            low = lax.rem(lane, 2 * d) < d
+            rim = jnp.where(
+                low,
+                loose(rims[self.e, 0, 0:size], self.groups),
+                loose(rims[self.e, 1, 0:size], self.groups),
+            )
+            rim = jnp.where(lane < 2 * d * ROWS, rim, 0.0)
+            left = right = 0.0
+            for a, shift in ((1, 0), (2, 2 * d * d), (0, LANES - 2 * d * d)):
+                moved = (pltpu.roll(rim, shift, 1) if shift else rim).astype(BF)
+                left = left + dot(v_side[l, a, :, 0:C], moved)
+                right = right + dot(v_side[l, a, :, C : 2 * C], moved)
+            both = jnp.where(low, left, right)
+            edge = both
+            for r in range(ROWS):
+                after = pltpu.roll(both, (-2 * d * (r + 1)) % LANES, 1)
+                acc[:, columns(r)] += jnp.where(
+                    lane < d, edge, jnp.where(lane >= LANES - d, after, 0.0)
+                )
+                edge = after
+
         def receive_corners(self):
             for slot, (away, copy) in enumerate(self.turns):
 
@@ -377,7 +405,7 @@
             return copy
 
         def around(axis):
-            for step in (1, 2, 3):
+            for step in (2, 1, 3):
                 to = lax.rem(coordinate(me, axis) + step, 4)
                 yield step - 1, to, with_coordinate(me, axis, to)
 
@@ -447,22 +475,32 @@
         store(full.at[l], dw_hbm.at[l])
         yield
 
-    def weight_sums(l, delta, stored):
-        d = 2**l
-        rest = CELLS - d * LANES
+    def block_sums(l, first, last):
+        delta, stored = backward_buffers[l], forward_buffers[l]
         for a in range(3):
-            partial[l, :, a * WIDE + 512 : (a + 1) * WIDE] = jnp.zeros((C, LANES), F32)
-        partial[l, :, 0:576] = dot_nt(delta[0:C, d * LANES : CELLS], stored[:, 0:rest])
-        partial[l, :, 640:1216] = dot_nt(delta[0:C, 0:CELLS], stored[:, 0:CELLS])
-        partial[l, :, 1280:1856] = dot_nt(
-            delta[0:C, 0:CELLS], stored[:, d * LANES : CELLS + d * LANES]
-        )
-        partial[l, :, 1920:2048] = jnp.broadcast_to(
+            shift = (a - 1) * 2**l * LANES
+            low = max(first, -shift)
+            block = dot_nt(delta[0:C, low:last], stored[:, low + shift : last + shift])
+            if first == 0:
+                partial[l, :, a * WIDE + 512 : (a + 1) * WIDE] = jnp.zeros((C, LANES), F32)
+                partial[l, :, a * WIDE : a * WIDE + 3 * C] = block
+            else:
+                partial[l, :, a * WIDE : a * WIDE + 3 * C] += block
+
+    def weight_sums(l):
+        block_sums(l, 0 if l > 0 else 6 * LANES, CELLS)
+        delta = backward_buffers[l]
+        partial[l, :, 3 * WIDE : TOTAL] = jnp.broadcast_to(
             jnp.sum(delta[0:C, 0:CELLS].astype(F32), axis=1, keepdims=True), (C, LANES)
         )
         reduction = all_reduce(l)
         next(reduction)
         return reduction
+
+    def cells_first(rows, cells):
+        for r in range(ROWS):
+            spread_rows[pl.ds(r, C, stride=ROWS), :] = rows[r].astype(F32)
+        cells[...] = spread_rows[...].reshape(C, ROWS, LANES).astype(BF)
 
     def prepare_forward(l):
         for a in range(3):
@@ -696,34 +734,35 @@
     rim.pack_sides(ROWS - d, ROWS)
     rim.send_sides()
 
-    store(out_ref, out_hbm)
     reductions = {}
     for l in (2, 1, 0):
         d = 2**l
         rest = CELLS - d * LANES
-        stored = forward_buffers[l]
         buf = backward_buffers[l]
         if l == 0:
-            reductions[0] = weight_sums(0, buf, stored)
+            reductions[0] = weight_sums(0)
             rim.pack_sides(0, ROWS)
             rim.send_sides()
             for older in (0, 1, 2):
                 next(reductions[older])
         else:
-            reductions[l] = weight_sums(l, buf, stored)
+            reductions[l] = weight_sums(l)
             for older in range(l + 1, 3):
                 next(reductions[older])
         acc[...] = dot(v_mid[l, 1], buf[0:C, 0:CELLS])
         acc[:, d * LANES : CELLS] += dot(v_mid[l, 2], buf[0:C, 0:rest])
         acc[:, 0:rest] += dot(v_mid[l, 0], buf[0:C, d * LANES : CELLS])
         rim.roll_sides()
-        rim.receive_sides()
+        acc[...] += dot(v_side[l, 1], buf[C : 3 * C, 0:CELLS])
+        acc[:, d * LANES : CELLS] += dot(v_side[l, 2], buf[C : 3 * C, 0:rest])
+        acc[:, 0:rest] += dot(v_side[l, 0], buf[C : 3 * C, d * LANES : CELLS])
+        if l == 2:
+            cells_first(out_ref, x_ref)
+            store(x_ref, out_hbm)
+        rim.receive_edges(l)
         if l == 0:
             for older in (0, 1, 2):
                 next(reductions[older])
-        acc[...] += dot(v_side[l, 1], buf[C : 3 * C, 0:CELLS])
-        acc[:, d * LANES : CELLS] += dot(v_side[l, 2], buf[C : 3 * C, 0:rest])
-        acc[:, 0:rest] += dot(v_side[l, 0], buf[C : 3 * C, d * LANES : CELLS])
 
         def descend(first, last):
             g = mask * (grad[:, first:last] + acc[:, first:last])
@@ -739,6 +778,8 @@
         descend(0, rest)
         if l > 0:
             next(reductions[l])
+        if l == 1:
+            block_sums(0, 0, 6 * LANES)
         rim.receive_corners()
         middle = d // 2
         for number, (fold, first, last) in enumerate(rim.folds):
@@ -764,7 +805,8 @@
             rim.pack_sides(0, ROWS)
             rim.send_sides()
 
-    store(fg_ref, fg_hbm)
+    cells_first(fg_ref, ct_ref)
+    store(ct_ref, fg_hbm)
     done = object()
     running = [reductions[l] for l in range(3)]
     while running:
@@ -783,16 +825,14 @@
 
 
 def finish(
-    rows_a,
-    rows_b,
+    cells_a,
+    cells_b,
     summed,
     out_a,
     out_b,
     kernel_grad,
     bias_grad,
-    rows,
     sums,
-    spread_rows,
     cells,
     kernels,
     bias_rows,
@@ -800,8 +840,8 @@
     out_sem,
 ):
     loads = [pltpu.make_async_copy(summed.at[l], sums.at[l], in_sem.at[l]) for l in range(3)]
-    for number, src in enumerate((rows_a, rows_b)):
-        loads.append(pltpu.make_async_copy(src, rows.at[number], in_sem.at[3 + number]))
+    for number, src in enumerate((cells_a, cells_b)):
+        loads.append(pltpu.make_async_copy(src, cells.at[number], in_sem.at[3 + number]))
     for load in loads:
         load.start()
     stores = []
@@ -813,6 +853,9 @@
 
     for l in range(3):
         loads[l].wait()
+        if l > 0:
+            loads[2 + l].wait()
+            store(cells.at[l - 1], (out_a, out_b)[l - 1])
         for a in range(3):
             for b in range(3):
                 first = a * WIDE + (1, 0, 2)[b] * C
@@ -821,12 +864,6 @@
             store(kernels.at[l, taps], kernel_grad.at[l, taps])
         bias_rows[l : l + 1, :] = sums[l, :, 3 * WIDE : TOTAL].astype(F32).T[0:1]
     store(bias_rows, bias_grad)
-    for number, dst in enumerate((out_a, out_b)):
-        loads[3 + number].wait()
-        for r in range(ROWS):
-            spread_rows[pl.ds(r, C, stride=ROWS), :] = rows[number, r].astype(F32)
-        cells[number] = spread_rows[...].reshape(C, ROWS, LANES).astype(BF)
-        store(cells.at[number], dst)
     for copy in stores:
         copy.wait()
 
@@ -837,8 +874,8 @@
     out, field_grad, summed = pl.pallas_call(
         functools.partial(kernel, n),
         out_shape=(
-            jax.ShapeDtypeStruct((ROWS, C, LANES), BF),
-            jax.ShapeDtypeStruct((ROWS, C, LANES), BF),
+            jax.ShapeDtypeStruct((C, ROWS, LANES), BF),
+            jax.ShapeDtypeStruct((C, ROWS, LANES), BF),
             jax.ShapeDtypeStruct((3, C, TOTAL), BF),
         ),
         in_specs=[
@@ -916,9 +953,7 @@
         in_specs=[hbm] * 3,
         out_specs=(hbm,) * 4,
         scratch_shapes=[
-            pltpu.VMEM((2, ROWS, C, LANES), BF),
             pltpu.VMEM((3, C, TOTAL), BF),
-            pltpu.VMEM((C * ROWS, LANES), F32),
             pltpu.VMEM((2, C, ROWS, LANES), BF),
             pltpu.VMEM((3, 9, C, C), F32),
             pltpu.VMEM((3, C), F32),

time: 82.5 us -> 80.9 us (0.981)
  Pallas kernels: 81 us -> 79.3 us
    pallas_call x1, Pallas kernels: 77 us -> 75.3 us  [shards(): pl.pallas_call(functools.partial(kernel, n), out_shape=(jax.ShapeDtypeStr...]
where the time goes in v7:
time: 80.9 us; the launch traced here: 80.8 us
  Pallas kernels  79.3 us (98%)
  between operations  1.45 us (2%)
    pallas_call x1, Pallas kernels, shards(): pl.pallas_call(functools.partial(kernel, n), out_shape=(jax.ShapeDtypeStr...  75.3 us
    pallas_call x1, Pallas kernels, shards(): pl.pallas_call(finish, out_shape=(jax.ShapeDtypeStruct((C, ROWS, LANES),...  3.98 us

profile of v7, /device:TPU:1, one launch (start us, length us, event | category | flops | bytes accessed | tf_op | source)
XLA Modules:
  0.0 80.8 jit_solution(2263471705169955630)
XLA Ops:
  1.3 75.3 %shard_map.93 = (bf16[192,8,128]{2,1,0:T(8,128)(2,1)}, bf16[192,8,128]{2,1,0:T(8,128)(2,1)}, bf16[3,192,2048]{2,1,0:T(8,128)(2,1)}) custom-call(bf16[192,8,128]{2,1,0:T(8,128)(2,1)} %x_hbm.1, bf16[192,8,128]{2,1,0:T(8,128)(2,1)} %ct_hbm.1, bf16[3,9,192,192]{3,2,1,0:T(8,128)(2,1)} %w_hbm.1, f32[3,192]{1,0:T(4,128)} %bias_hbm.1, s32[1,1]{1,0:T(1,128)S(6)} %copy.10.ocean_ref, ...), custom_call_target="tpu_custom_call" | custom-call | flops 6115295232 | bytes 8388608 | tf_op jit(solution)/shard_map/pallas_call | solution.py:874
  76.6 4.0 %shard_map.94 = (bf16[192,8,128]{2,1,0:T(8,128)(2,1)}, bf16[192,8,128]{2,1,0:T(8,128)(2,1)}, f32[3,9,192,192]{3,2,1,0:T(8,128)}, f32[3,192]{1,0:T(4,128)}) custom-call(bf16[192,8,128]{2,1,0:T(8,128)(2,1)} %get-tuple-element.7.cells_a, bf16[192,8,128]{2,1,0:T(8,128)(2,1)} %get-tuple-element.8.cells_b, bf16[3,192,2048]{2,1,0:T(8,128)(2,1)} %get-tuple-element.9.summed), custom_call_target="tpu_custom_call" | custom-call | tf_op jit(solution)/shard_map/pallas_call | solution.py:945

commit v8 on v7

--- a/solution.py
+++ b/solution.py
@@ -533,21 +533,6 @@
     tile = slots(lambda k: turned[0, :, columns(k)], 3)
     tile = jnp.where(jnp.logical_and(lane >= 24, lane < 32), mask, tile)
     corner[0] = dense(tile, 4)
-    loads[0].wait()
-    prepare_forward(0)
-    for a in range(3):
-        for place, b in enumerate((1, 0, 2)):
-            part = slice(place * C, (place + 1) * C)
-            w_own[a, :, part] = w_ref[0, 3 * a + b]
-            w_turn[a, :, part] = (w_ref[0, 8 - 3 * a - b].astype(F32) * cols_ref[3:4, 0:C]).astype(
-                BF
-            )
-    small[3].wait()
-    spread_rows[...] = ct_ref[...].astype(F32).reshape(C * ROWS, LANES)
-    for r in range(ROWS):
-        grad[:, columns(r)] = mask * spread_rows[pl.ds(r, C, stride=ROWS), :]
-    loads[1].wait()
-    loads[2].wait()
     pl.semaphore_wait(
         barrier, len(partners) + a_away.astype(jnp.int32) + b_away.astype(jnp.int32)
     )
@@ -583,6 +568,21 @@
                 out_ref[r] = after[:, r * LANES - first : (r + 1) * LANES - first].astype(BF)
             t2[0:C, first:last] = (grad[:, first:last] * s).astype(BF)
 
+    loads[0].wait()
+    prepare_forward(0)
+    for a in range(3):
+        for place, b in enumerate((1, 0, 2)):
+            part = slice(place * C, (place + 1) * C)
+            w_own[a, :, part] = w_ref[0, 3 * a + b]
+            w_turn[a, :, part] = (w_ref[0, 8 - 3 * a - b].astype(F32) * cols_ref[3:4, 0:C]).astype(
+                BF
+            )
+    small[3].wait()
+    spread_rows[...] = ct_ref[...].astype(F32).reshape(C * ROWS, LANES)
+    for r in range(ROWS):
+        grad[:, columns(r)] = mask * spread_rows[pl.ds(r, C, stride=ROWS), :]
+    loads[1].wait()
+    loads[2].wait()
     rest = CELLS - LANES
     acc[...] = dot(w_ref[0, 4], s0[0:C, 0:CELLS]) + bias_cols[0]
     acc[:, 0:rest] += dot(w_ref[0, 7], s0[0:C, LANES:CELLS])
@@ -672,9 +672,11 @@
         )
         activate(1, s1, first, last)
 
-    second(0, 4 * LANES)
+    second(0, 5 * LANES)
     later = Rims(2, s2, 4, True)
-    later.pack_sides(0, 4)
+    later.turn(3, 4)
+    later.send_fold(3, 4)
+    later.pack_sides(0, 5)
     prepare_forward(2)
 
     rim.folds[0][0].wait_recv()
@@ -692,14 +694,14 @@
     s1[0:C, columns(ROWS, 2)] = (far_mask * (s0[0:C, columns(ROWS, 2)].astype(F32) + v)).astype(BF)
     for r in range(ROWS - 1, ROWS + 2):
         widen(s1, next_tile, r, 2)
-    second(4 * LANES, CELLS)
+    second(5 * LANES, CELLS)
     rim = later
-    rim.turn(0, 4)
+    rim.turn(0, 3)
     rim.pack_corners()
     rim.send_corners()
     rim.send_fold(0, 2)
-    rim.send_fold(2, 4)
-    rim.pack_sides(4, ROWS)
+    rim.send_fold(2, 3)
+    rim.pack_sides(5, ROWS)
     rim.send_sides()
 
     d = 4
@@ -718,14 +720,15 @@
     later = Rims(3, t2, d, False)
     later.pack_sides(0, ROWS - d)
     rim.receive_corners()
-    for number, (fold, first, last) in enumerate(rim.folds):
-        rim.receive_fold(number)
+    for first, last, numbers in ((0, 2, (1,)), (2, 4, (2, 0))):
+        for number in numbers:
+            rim.receive_fold(number)
         top = slice(rest + first * LANES, rest + last * LANES)
         over = slice(CELLS + first * LANES, CELLS + last * LANES)
         acc[:, top] += dot(w_ref[2, 7], s2[0:C, over]) + dot(w_side[2, 2], s2[C : 3 * C, over])
         activate(2, s2, top.start, top.stop)
         later.turn(d - last, d - first)
-        if number == 0:
+        if first == 0:
             later.send_fold(d - last, d - first)
     rim = later
     rim.pack_corners()
@@ -930,8 +933,8 @@
             pltpu.VMEM((3, C, TOTAL), BF),
             pltpu.SemaphoreType.DMA((7,)),
             pltpu.SemaphoreType.DMA((5,)),
-            pltpu.SemaphoreType.DMA((6, 6)),
-            pltpu.SemaphoreType.DMA((6, 6)),
+            pltpu.SemaphoreType.DMA((6, 7)),
+            pltpu.SemaphoreType.DMA((6, 7)),
             pltpu.SemaphoreType.DMA((3, 40)),
             pltpu.SemaphoreType.DMA((3, 40)),
         ],

time: 80.9 us -> 80.2 us (level)
  no operation moved by 1% of the time
where the time goes in v8:
time: 80.2 us; the launch traced here: 80.1 us
  Pallas kernels  78.7 us (98%)
  between operations  1.45 us (2%)
    pallas_call x1, Pallas kernels, shards(): pl.pallas_call(functools.partial(kernel, n), out_shape=(jax.ShapeDtypeStr...  74.7 us
    pallas_call x1, Pallas kernels, shards(): pl.pallas_call(finish, out_shape=(jax.ShapeDtypeStruct((C, ROWS, LANES),...  3.98 us

profile of v8, /device:TPU:1, one launch (start us, length us, event | category | flops | bytes accessed | tf_op | source)
XLA Modules:
  0.0 80.1 jit_solution(4250616500365902496)
XLA Ops:
  1.3 74.7 %shard_map.93 = (bf16[192,8,128]{2,1,0:T(8,128)(2,1)}, bf16[192,8,128]{2,1,0:T(8,128)(2,1)}, bf16[3,192,2048]{2,1,0:T(8,128)(2,1)}) custom-call(bf16[192,8,128]{2,1,0:T(8,128)(2,1)} %x_hbm.1, bf16[192,8,128]{2,1,0:T(8,128)(2,1)} %ct_hbm.1, bf16[3,9,192,192]{3,2,1,0:T(8,128)(2,1)} %w_hbm.1, f32[3,192]{1,0:T(4,128)} %bias_hbm.1, s32[1,1]{1,0:T(1,128)S(6)} %copy.10.ocean_ref, ...), custom_call_target="tpu_custom_call" | custom-call | flops 6115295232 | bytes 8388608 | tf_op jit(solution)/shard_map/pallas_call | solution.py:877
  76.0 4.0 %shard_map.94 = (bf16[192,8,128]{2,1,0:T(8,128)(2,1)}, bf16[192,8,128]{2,1,0:T(8,128)(2,1)}, f32[3,9,192,192]{3,2,1,0:T(8,128)}, f32[3,192]{1,0:T(4,128)}) custom-call(bf16[192,8,128]{2,1,0:T(8,128)(2,1)} %get-tuple-element.7.cells_a, bf16[192,8,128]{2,1,0:T(8,128)(2,1)} %get-tuple-element.8.cells_b, bf16[3,192,2048]{2,1,0:T(8,128)(2,1)} %get-tuple-element.9.summed), custom_call_target="tpu_custom_call" | custom-call | tf_op jit(solution)/shard_map/pallas_call | solution.py:948

commit v9 on v8

--- a/solution.py
+++ b/solution.py
@@ -164,7 +164,7 @@
     loads = [
         pltpu.make_async_copy(w_hbm.at[l], w_ref.at[l], w_sem.at[l]) for l in range(3)
     ]
-    for load in small + loads:
+    for load in small[2:3] + small[:2] + loads[:1] + small[3:] + loads[1:]:
         load.start()
 
     lane = lax.broadcasted_iota(jnp.int32, (C, LANES), 1)
@@ -854,6 +854,7 @@
         copy.start()
         stores.append(copy)
 
+    biases = []
     for l in range(3):
         loads[l].wait()
         if l > 0:
@@ -865,7 +866,8 @@
                 kernels[l, 3 * a + b] = sums[l, :, first : first + C].astype(F32)
             taps = pl.ds(3 * a, 3)
             store(kernels.at[l, taps], kernel_grad.at[l, taps])
-        bias_rows[l : l + 1, :] = sums[l, :, 3 * WIDE : TOTAL].astype(F32).T[0:1]
+        biases.append(sums[l, :, 3 * WIDE : TOTAL].astype(F32).T[0:1])
+    bias_rows[...] = jnp.concatenate(biases, axis=0)
     store(bias_rows, bias_grad)
     for copy in stores:
         copy.wait()

time: 80.2 us -> 79.9 us (level)
  no operation moved by 1% of the time
where the time goes in v9:
time: 79.9 us; the launch traced here: 79.8 us
  Pallas kernels  78.3 us (98%)
  between operations  1.45 us (2%)
    pallas_call x1, Pallas kernels, shards(): pl.pallas_call(functools.partial(kernel, n), out_shape=(jax.ShapeDtypeStr...  74.4 us
    pallas_call x1, Pallas kernels, shards(): pl.pallas_call(finish, out_shape=(jax.ShapeDtypeStruct((C, ROWS, LANES),...  3.98 us

profile of v9, /device:TPU:1, one launch (start us, length us, event | category | flops | bytes accessed | tf_op | source)
XLA Modules:
  0.0 79.8 jit_solution(13681777611416120699)
XLA Ops:
  1.3 74.4 %shard_map.93 = (bf16[192,8,128]{2,1,0:T(8,128)(2,1)}, bf16[192,8,128]{2,1,0:T(8,128)(2,1)}, bf16[3,192,2048]{2,1,0:T(8,128)(2,1)}) custom-call(bf16[192,8,128]{2,1,0:T(8,128)(2,1)} %x_hbm.1, bf16[192,8,128]{2,1,0:T(8,128)(2,1)} %ct_hbm.1, bf16[3,9,192,192]{3,2,1,0:T(8,128)(2,1)} %w_hbm.1, f32[3,192]{1,0:T(4,128)} %bias_hbm.1, s32[1,1]{1,0:T(1,128)S(6)} %copy.10.ocean_ref, ...), custom_call_target="tpu_custom_call" | custom-call | flops 6115295232 | bytes 8388608 | tf_op jit(solution)/shard_map/pallas_call | solution.py:879
  75.6 4.0 %shard_map.94 = (bf16[192,8,128]{2,1,0:T(8,128)(2,1)}, bf16[192,8,128]{2,1,0:T(8,128)(2,1)}, f32[3,9,192,192]{3,2,1,0:T(8,128)}, f32[3,192]{1,0:T(4,128)}) custom-call(bf16[192,8,128]{2,1,0:T(8,128)(2,1)} %get-tuple-element.7.cells_a, bf16[192,8,128]{2,1,0:T(8,128)(2,1)} %get-tuple-element.8.cells_b, bf16[3,192,2048]{2,1,0:T(8,128)(2,1)} %get-tuple-element.9.summed), custom_call_target="tpu_custom_call" | custom-call | tf_op jit(solution)/shard_map/pallas_call | solution.py:950
